TPU v7x, 32 devices: a whole 2x2x4 slice. The times are simulated.
32 devices in a mesh: group: 8 (over z, x), mp: 4 (over y, core).
Axes of the slice: x: 2, y: 2, z: 4, core: 2. Of those that a mesh axis runs over, the one named last changes fastest.
Arguments:
- tokens: bfloat16 [8192, 2048], P('group', 'mp'), may hold values from -6 to 6
- in_gain: float32 [2048], replicated, may hold values from 0.5 to 1.5
- trainer_qkv: float32 [2048, 6144], P(('group', 'mp')), may hold values from -0.125 to 0.125
- head_order: int32 [16], replicated, may hold values from 0 to 15, each once
- conv_weight: float32 [4, 6144], P(None, 'mp'), may hold values from -3 to 3
- beta_weight: bfloat16 [2048, 16], P(None, 'mp'), may hold values from -0.125 to 0.125
- beta_bias: float32 [16], P('mp'), may hold values from -4 to 3
- out_gain: float32 [128], replicated, may hold values from 0.5 to 1.5
- lengths: int32 [8, 8], P('group'), may hold values from 1 to 8, 16 in all within a row
- prior_states: float32 [64, 16, 128, 128], P('group', 'mp'), may hold values from -0.6 to 0.6
- page_table: int32 [64], P('group'), may hold values from 0 to 63, as said below
- o_weight: bfloat16 [2048, 2048], P('mp', 'group'), may hold values from -0.1875 to 0.1875
- gate_weight: bfloat16 [2048, 5632], P('group', 'mp'), may hold values from -0.125 to 0.125
- up_weight: bfloat16 [2048, 5632], P('group', 'mp'), may hold values from -0.125 to 0.125
- down_weight: bfloat16 [5632, 2048], P('mp', 'group'), may hold values from -0.109375 to 0.109375
Outputs:
- attended: bfloat16 [8192, 2048], P('group', 'mp')
- state_pages: float32 [64, 16, 128, 128], P('group', 'mp')
- layer_out: bfloat16 [8192, 2048], P('group', 'mp')
Inputs may be any that keep to these rules, and one draw needn't show every extreme that they name: lengths count blocks of 64 tokens; the lengths of one group sum to 16; the longest of each group is 8. `page_table`: a permutation of the 64 pages; page p lies on group p // 8; the 8 slots of one group name pages of exactly 4 groups, exactly 2 pages of each.
All inputs are finite; a program needn't handle non-finite values.
Results may differ from a plain program's by a relative error of at most 0.018.
Values may be sent and summed in bfloat16 or wider, within the bound.
A program may use at most 128 MiB of HBM per device.

v0:
```python
from functools import partial

import jax
import jax.numpy as jnp
from jax import lax
from jax.sharding import PartitionSpec as P

SPAN = 64


EPSILON = 1e-06


def from_behind(value, axis, steps):
    count = lax.axis_size(axis)
    initial, last = (max(0, -steps), min(count, count - steps))
    return lax.ppermute(value, axis, [(source, source + steps) for source in range(initial, last)])


def unit_rows(matrix):
    return matrix * lax.rsqrt(jnp.sum(matrix * matrix, axis=-1, keepdims=True) + EPSILON)


def normalize_rows(matrix, scaling):
    widened = matrix.astype(jnp.float32)
    return (
        widened * lax.rsqrt(jnp.mean(widened * widened, axis=-1, keepdims=True) + EPSILON) * scaling
    )


def segment_layout(lengths_row, span_total, span_rows):
    starts = jnp.cumsum(lengths_row) - lengths_row
    span_ids = jnp.arange(span_total, dtype=jnp.int32)
    seg_of_span = jnp.sum((span_ids[:, None] >= starts[None, :]).astype(jnp.int32), axis=1) - 1
    is_start = jnp.any(span_ids[:, None] == starts[None, :], axis=1)
    positions = jnp.arange(span_total * span_rows, dtype=jnp.int32)
    token_seg = jnp.repeat(seg_of_span, span_rows)
    offset = positions - jnp.take(starts, token_seg) * span_rows
    return (starts, seg_of_span, is_start, token_seg, offset)


def convolve(rows_wide, history, weight, offset, token_seg):
    row_total = rows_wide.shape[0]
    tap_count = weight.shape[0]
    extended = jnp.concatenate([history, rows_wide], axis=0)
    summed = jnp.zeros(rows_wide.shape, jnp.float32)
    for lag_index in range(tap_count):
        lagged = (
            extended[tap_count - 1 - lag_index : tap_count - 1 - lag_index + row_total]
            * weight[lag_index]
        )
        permitted_mask = (offset >= lag_index) | (token_seg == 0)
        summed = summed + jnp.where(permitted_mask[:, None], lagged, 0.0)
    return summed


def prepare(span_block, key_feature_width):
    active = jax.nn.silu(span_block)
    row_total = span_block.shape[0]
    split_rows = active.reshape(row_total, -1, 3, key_feature_width).transpose(1, 2, 0, 3)
    query_matrix = unit_rows(split_rows[:, 0]) * key_feature_width ** (-0.5)
    lookup_entries_by_token = unit_rows(split_rows[:, 1])
    value_rows = split_rows[:, 2]
    return (query_matrix, lookup_entries_by_token, value_rows)


def span_step(carried_summary_memory, query_matrix, lookup_entries_by_token, value_rows, gating):
    numeric_accuracy_mode = lax.Precision.HIGHEST
    row_total = query_matrix.shape[1]
    key_feature_width = lookup_entries_by_token.shape[2]
    strict = jnp.tril(jnp.ones((row_total, row_total), jnp.float32), -1)
    inclusive = jnp.tril(jnp.ones((row_total, row_total), jnp.float32))
    gram = jnp.einsum(
        "hik,hjk->hij",
        lookup_entries_by_token,
        lookup_entries_by_token,
        precision=numeric_accuracy_mode,
    )
    system = jnp.eye(row_total, dtype=jnp.float32) + gating[:, :, None] * gram * strict
    solve_target_vector = (
        jnp.concatenate([lookup_entries_by_token, value_rows], axis=2) * gating[:, :, None]
    )
    solution_matrix = lax.linalg.triangular_solve(
        system, solve_target_vector, left_side=True, lower=True
    )
    corrected_content_entries = solution_matrix[:, :, key_feature_width:] - jnp.einsum(
        "xsi,xin->xsn",
        solution_matrix[:, :, :key_feature_width],
        carried_summary_memory,
        precision=numeric_accuracy_mode,
    )
    attention_scores = (
        jnp.einsum(
            "hik,hjk->hij", query_matrix, lookup_entries_by_token, precision=numeric_accuracy_mode
        )
        * inclusive
    )
    output_matrix_rows = jnp.einsum(
        "xsi,xin->xsn", query_matrix, carried_summary_memory, precision=numeric_accuracy_mode
    ) + jnp.einsum(
        "pzd,pdu->pzu", attention_scores, corrected_content_entries, precision=numeric_accuracy_mode
    )
    carried_summary_memory = carried_summary_memory + jnp.einsum(
        "jtc,jtb->jcb",
        lookup_entries_by_token,
        corrected_content_entries,
        precision=numeric_accuracy_mode,
    )
    return (output_matrix_rows, carried_summary_memory)


def span_at(
    span_index,
    carried_summary_memory,
    initial,
    convolved,
    gating_all,
    seg_of_span,
    is_start,
    span_rows,
    key_feature_width,
):
    span_block = lax.dynamic_slice_in_dim(convolved, span_index * span_rows, span_rows, 0)
    gating = lax.dynamic_slice_in_dim(gating_all, span_index * span_rows, span_rows, 0).T
    opening = initial[seg_of_span[span_index]]
    carried_summary_memory = jnp.where(is_start[span_index], opening, carried_summary_memory)
    query_matrix, lookup_entries_by_token, value_rows = prepare(span_block, key_feature_width)
    return span_step(
        carried_summary_memory, query_matrix, lookup_entries_by_token, value_rows, gating
    )


def shards(
    tokens,
    in_gain,
    trainer_qkv,
    head_order,
    conv_weight,
    beta_weight,
    beta_bias,
    out_gain,
    lengths,
    prior_states,
    page_table,
    o_weight,
    gate_weight,
    up_weight,
    down_weight,
):
    numeric_accuracy_mode = lax.Precision.HIGHEST
    mp_count = lax.axis_size("mp")
    group_count = lax.axis_size("group")
    head_total = head_order.shape[0]
    local_heads = head_total // mp_count
    key_feature_width = prior_states.shape[2]
    joined_width = 3 * key_feature_width
    share_rows = trainer_qkv.shape[0]
    gathered = lax.all_gather(tokens, "mp", axis=1, tiled=True)
    token_total = gathered.shape[0]
    normed = normalize_rows(gathered, in_gain).astype(jnp.bfloat16)
    ordered = jnp.take(
        trainer_qkv.reshape(share_rows, head_total, joined_width), jnp.argsort(head_order), axis=1
    ).astype(jnp.bfloat16)
    trainer_rows = lax.all_gather(ordered, "group", axis=0, tiled=True)
    head_split = lax.all_to_all(trainer_rows, "mp", split_axis=1, concat_axis=0, tiled=True)
    arranged = (
        head_split.reshape(mp_count, group_count, share_rows, local_heads * joined_width)
        .transpose(1, 0, 2, 3)
        .reshape(-1, local_heads * joined_width)
    )
    projected = jnp.dot(normed, arranged, preferred_element_type=jnp.float32).astype(jnp.bfloat16)
    gating_all = jax.nn.sigmoid(
        jnp.dot(normed, beta_weight, preferred_element_type=jnp.float32) + beta_bias
    )
    span_total = token_total // SPAN
    starts, seg_of_span, is_start, token_seg, offset = segment_layout(lengths[0], span_total, SPAN)
    taps_less = conv_weight.shape[0] - 1
    expanded_hidden_lift = projected.astype(jnp.float32)
    convolved = convolve(
        expanded_hidden_lift,
        jnp.zeros((taps_less, projected.shape[1]), jnp.float32),
        conv_weight,
        offset,
        token_seg,
    )

    def advance(span_index, loop_state, initial, source):
        outputs, memories, carried_summary_memory = loop_state
        output_matrix_rows, carried_summary_memory = span_at(
            span_index,
            carried_summary_memory,
            initial,
            source,
            gating_all,
            seg_of_span,
            is_start,
            SPAN,
            key_feature_width,
        )
        outputs = lax.dynamic_update_index_in_dim(outputs, output_matrix_rows, span_index, 0)
        memories = lax.dynamic_update_index_in_dim(memories, carried_summary_memory, span_index, 0)
        return (outputs, memories, carried_summary_memory)

    blank = jnp.zeros((local_heads, key_feature_width, key_feature_width), jnp.float32)
    loop_state = (
        jnp.zeros((span_total, local_heads, SPAN, key_feature_width), jnp.float32),
        jnp.zeros((span_total, local_heads, key_feature_width, key_feature_width), jnp.float32),
        blank,
    )
    last_start = starts[-1]
    outputs, memories, carried_summary_memory = lax.fori_loop(
        last_start,
        jnp.int32(span_total),
        partial(advance, initial=prior_states, source=convolved),
        loop_state,
    )
    got_memory, got_rows = (
        from_behind(memories[span_total - 1].astype(jnp.bfloat16), "group", 1).astype(jnp.float32),
        from_behind(
            expanded_hidden_lift[token_total - taps_less :].astype(jnp.bfloat16), "group", 1
        ).astype(jnp.float32),
    )
    linked = lax.axis_index("group") > 0
    history = jnp.where(linked, got_rows, 0.0)
    head_rows = convolve(
        expanded_hidden_lift[:taps_less],
        history,
        conv_weight,
        offset[:taps_less],
        token_seg[:taps_less],
    )
    convolved = lax.dynamic_update_slice_in_dim(convolved, head_rows, 0, 0)
    initial = prior_states.at[0].set(jnp.where(linked, got_memory, prior_states[0]))
    outputs, memories, carried_summary_memory = lax.fori_loop(
        jnp.int32(0),
        last_start,
        partial(advance, initial=initial, source=convolved),
        (outputs, memories, blank),
    )
    mixed = outputs.transpose(0, 2, 1, 3).reshape(token_total, local_heads, key_feature_width)
    attended = (
        normalize_rows(mixed, out_gain)
        .astype(jnp.bfloat16)
        .reshape(token_total, local_heads * key_feature_width)
    )
    last_spans = starts + lengths[0] - 1
    finals = jnp.take(memories, last_spans, axis=0).reshape(last_spans.shape[0], -1)
    req_count = page_table.shape[0]
    my_group = lax.axis_index("group")
    wanted_ids = my_group * req_count + jnp.arange(req_count, dtype=jnp.int32)
    piece_states = lax.all_gather(finals.astype(jnp.bfloat16), "group", axis=0, tiled=True).astype(
        jnp.float32
    )
    piece_ids = lax.all_gather(page_table, "group", axis=0, tiled=True)
    picker = (piece_ids[None, :] == wanted_ids[:, None]).astype(jnp.float32)
    placed = jnp.zeros(finals.shape, jnp.float32) + jnp.dot(
        picker, piece_states, precision=numeric_accuracy_mode
    )
    state_pages = placed.reshape(prior_states.shape)
    mixer_terms = jnp.dot(
        attended,
        lax.all_gather(o_weight, "group", axis=1, tiled=True),
        preferred_element_type=jnp.float32,
    ).astype(jnp.bfloat16)
    mixer_terms = lax.optimization_barrier(mixer_terms).astype(jnp.float32)
    mixer_sum = lax.psum_scatter(
        mixer_terms.astype(jnp.bfloat16), "mp", scatter_dimension=1, tiled=True
    ).astype(jnp.float32)
    residual_one = (tokens.astype(jnp.float32) + mixer_sum).astype(jnp.bfloat16)
    mixed_rows = lax.all_gather(residual_one, "mp", axis=1, tiled=True)
    post_normed = normalize_rows(mixed_rows, 1.0).astype(jnp.bfloat16)
    gate_part = jnp.dot(
        post_normed,
        lax.all_gather(gate_weight, "group", axis=0, tiled=True),
        preferred_element_type=jnp.float32,
    )
    up_part = jnp.dot(
        post_normed,
        lax.all_gather(up_weight, "group", axis=0, tiled=True),
        preferred_element_type=jnp.float32,
    )
    hidden = (jax.nn.silu(gate_part) * up_part).astype(jnp.bfloat16)
    feed_terms = jnp.dot(
        hidden,
        lax.all_gather(down_weight, "group", axis=1, tiled=True),
        preferred_element_type=jnp.float32,
    ).astype(jnp.bfloat16)
    feed_terms = lax.optimization_barrier(feed_terms).astype(jnp.float32)
    feed_sum = lax.psum_scatter(
        feed_terms.astype(jnp.bfloat16), "mp", scatter_dimension=1, tiled=True
    ).astype(jnp.float32)
    layer_out = (residual_one.astype(jnp.float32) + feed_sum).astype(jnp.bfloat16)
    return (attended, state_pages, layer_out)


def solution(mesh):
    in_specs = (
        P("group", "mp"),
        P(),
        P(("group", "mp"), None),
        P(),
        P(None, "mp"),
        P(None, "mp"),
        P("mp"),
        P(),
        P("group", None),
        P("group", "mp", None, None),
        P("group"),
        P("mp", "group"),
        P("group", "mp"),
        P("group", "mp"),
        P("mp", "group"),
    )
    out_specs = (P("group", "mp"), P("group", "mp", None, None), P("group", "mp"))
    return jax.shard_map(shards, mesh=mesh, in_specs=in_specs, out_specs=out_specs, check_vma=False)
```

profile of v0, /device:TPU:0, one launch (start us, length us, event | category | flops | bytes accessed | tf_op | source)
XLA Modules:
  0.0 1344.4 jit_solution(3206140579166413836)
XLA Ops:
  15.8 101.1 %all-gather.11.cloned.1.call-done = bf16[512,16,384]{2,0,1:T(8,128)(2,1)} async-done(((bf16[64,16,384]{2,0,1:T(8,128)(2,1)}), bf16[512,16,384]{2,0,1:T(8,128)(2,1)}) %all-gather.11.cloned.1.call-update) | async-done | bytes 6291472 | tf_op jit(solution)/shard_map/all_gather | solution.py:164
  131.8 41.9 %all-gather.9.cloned.1.call-done = bf16[1024,2048]{1,0:T(8,128)(2,1)} async-done(((bf16[1024,512]{1,0:T(8,128)(2,1)}), bf16[1024,2048]{1,0:T(8,128)(2,1)}) %all-gather.9.cloned.1.call-update) | async-done | bytes 4194320 | tf_op jit(solution)/shard_map/all_gather | solution.py:158
  178.4 36.9 %all-to-all-done = bf16[512,16,384]{2,0,1:T(8,128)(2,1)} async-done(((bf16[512,16,384]{2,0,1:T(8,128)(2,1)}), bf16[512,16,384]{2,0,1:T(8,128)(2,1)}, u32[]{:S(2)}, u32[]{:S(2)}) %all-to-all-start) | async-done | bytes 6291488 | tf_op jit(solution)/shard_map/all_to_all | solution.py:165
  257.4 29.9 %while.29 = (s32[]{:T(128)}, f32[16,4,64,128]{3,2,1,0:T(8,128)S(1)}, bf16[16,4,128,128]{3,2,1,0:T(8,128)(2,1)}, f32[4,128,128]{2,1,0:T(8,128)S(1)}, f32[1024,153...) while((s32[]{:T(128)}, ...), condition=%wide.region_8.10_spmd, body=%wide.region_5.9_spmd.sunk | while | flops 277950528 | bytes 7872302 | solution.py:211
  264.9 19.7 %custom-call.12 = f32[4,1,64,64]{2,3,1,0:T(8,128)S(1)} custom-call(f32[4,1,64,64]{3,2,1,0:T(8,128)S(1)} %fusion.181), custom_call_target="InvertDiagBlocksLowerTriangular" | custom-call | tf_op jit(solution)/shard_map/while/body/triangular_solve/custom-call.1 | solution.py:83
  292.2 32.7 %collective-permute-start.1 = (bf16[4,128,128]{2,1,0:T(8,128)(2,1)S(1)}, bf16[4,128,128]{2,1,0:T(8,128)(2,1)S(1)}, u32[]{:S(2)}, u32[]{:S(2)}) collective-permute-start(bf16[4,128,128]{2,1,0:T(8,128)(2,1)S(1)} %fusion.74), channel_id=1, source_target_pairs={{0,4},{4,8},{8,12},{12,16},{16,20},{20,24},{24,28},{1,5},{5,9},{9,... | collective-permute-start | bytes 393224 | tf_op jit(solution)/shard_map/ppermute | solution.py:17
  329.2 459.2 %while.30 = (s32[]{:T(128)}, f32[16,4,64,128]{3,2,1,0:T(8,128)S(1)}, bf16[16,4,128,128]{3,2,1,0:T(8,128)(2,1)}, f32[4,128,128]{2,1,0:T(8,128)S(1)}, s32[]{:T(128...) while((s32[]{:T(128)}, ...), condition=%wide.region_12.14_spmd, body=%wide.region_9.13_spmd.sunk | while | flops 277950528 | bytes 7872310 | solution.py:234
  337.3 19.7 %custom-call.13 = f32[4,1,64,64]{2,3,1,0:T(8,128)S(1)} custom-call(f32[4,1,64,64]{3,2,1,0:T(8,128)S(1)} %fusion.198), custom_call_target="InvertDiagBlocksLowerTriangular" | custom-call | tf_op jit(solution)/shard_map/while/body/triangular_solve/custom-call.1 | solution.py:83
  367.8 19.7 %custom-call.13 = f32[4,1,64,64]{2,3,1,0:T(8,128)S(1)} custom-call(f32[4,1,64,64]{3,2,1,0:T(8,128)S(1)} %fusion.198), custom_call_target="InvertDiagBlocksLowerTriangular" | custom-call | tf_op jit(solution)/shard_map/while/body/triangular_solve/custom-call.1 | solution.py:83
  398.4 19.7 %custom-call.13 = f32[4,1,64,64]{2,3,1,0:T(8,128)S(1)} custom-call(f32[4,1,64,64]{3,2,1,0:T(8,128)S(1)} %fusion.198), custom_call_target="InvertDiagBlocksLowerTriangular" | custom-call | tf_op jit(solution)/shard_map/while/body/triangular_solve/custom-call.1 | solution.py:83
  429.0 19.7 %custom-call.13 = f32[4,1,64,64]{2,3,1,0:T(8,128)S(1)} custom-call(f32[4,1,64,64]{3,2,1,0:T(8,128)S(1)} %fusion.198), custom_call_target="InvertDiagBlocksLowerTriangular" | custom-call | tf_op jit(solution)/shard_map/while/body/triangular_solve/custom-call.1 | solution.py:83
  459.5 19.7 %custom-call.13 = f32[4,1,64,64]{2,3,1,0:T(8,128)S(1)} custom-call(f32[4,1,64,64]{3,2,1,0:T(8,128)S(1)} %fusion.198), custom_call_target="InvertDiagBlocksLowerTriangular" | custom-call | tf_op jit(solution)/shard_map/while/body/triangular_solve/custom-call.1 | solution.py:83
  490.1 19.7 %custom-call.13 = f32[4,1,64,64]{2,3,1,0:T(8,128)S(1)} custom-call(f32[4,1,64,64]{3,2,1,0:T(8,128)S(1)} %fusion.198), custom_call_target="InvertDiagBlocksLowerTriangular" | custom-call | tf_op jit(solution)/shard_map/while/body/triangular_solve/custom-call.1 | solution.py:83
  520.7 19.7 %custom-call.13 = f32[4,1,64,64]{2,3,1,0:T(8,128)S(1)} custom-call(f32[4,1,64,64]{3,2,1,0:T(8,128)S(1)} %fusion.198), custom_call_target="InvertDiagBlocksLowerTriangular" | custom-call | tf_op jit(solution)/shard_map/while/body/triangular_solve/custom-call.1 | solution.py:83
  551.2 19.7 %custom-call.13 = f32[4,1,64,64]{2,3,1,0:T(8,128)S(1)} custom-call(f32[4,1,64,64]{3,2,1,0:T(8,128)S(1)} %fusion.198), custom_call_target="InvertDiagBlocksLowerTriangular" | custom-call | tf_op jit(solution)/shard_map/while/body/triangular_solve/custom-call.1 | solution.py:83
  581.8 19.7 %custom-call.13 = f32[4,1,64,64]{2,3,1,0:T(8,128)S(1)} custom-call(f32[4,1,64,64]{3,2,1,0:T(8,128)S(1)} %fusion.198), custom_call_target="InvertDiagBlocksLowerTriangular" | custom-call | tf_op jit(solution)/shard_map/while/body/triangular_solve/custom-call.1 | solution.py:83
  799.5 44.2 %reduce-scatter.3.cloned.1.call-done = bf16[1024,512]{1,0:T(8,128)(2,1)} async-done(((bf16[1024,2048]{1,0:T(8,128)(2,1)}), bf16[1024,512]{1,0:T(8,128)(2,1)}) %reduce-scatter.3.cloned.1.call-update) | async-done | bytes 1048592 | tf_op jit(solution)/shard_map/reduce_scatter | solution.py:266
  851.1 29.7 %all-gather.17.cloned.1.call-done = bf16[1024,2048]{1,0:T(8,128)(2,1)} async-done(((bf16[1024,512]{1,0:T(8,128)(2,1)}), bf16[1024,2048]{1,0:T(8,128)(2,1)}) %all-gather.17.cloned.1.call-update) | async-done | bytes 4194320 | tf_op jit(solution)/shard_map/all_gather | solution.py:270
  884.0 91.9 %all-gather.19.cloned.1.call-done = bf16[2048,1408]{1,0:T(8,128)(2,1)} async-done(((bf16[256,1408]{1,0:T(8,128)(2,1)}), bf16[2048,1408]{1,0:T(8,128)(2,1)}) %all-gather.19.cloned.1.call-update) | async-done | bytes 5767184 | tf_op jit(solution)/shard_map/all_gather | solution.py:274
  987.8 82.1 %all-gather.23.cloned.1.call-done = bf16[1408,2048]{1,0:T(8,128)(2,1)} async-done(((bf16[1408,256]{1,0:T(8,128)(2,1)}), bf16[1408,2048]{1,0:T(8,128)(2,1)}) %all-gather.23.cloned.1.call-update) | async-done | bytes 5767184 | tf_op jit(solution)/shard_map/all_gather | solution.py:285
  1069.9 93.3 %all-gather.21.cloned.1.call-done = bf16[2048,1408]{1,0:T(8,128)(2,1)} async-done(((bf16[256,1408]{1,0:T(8,128)(2,1)}), bf16[2048,1408]{1,0:T(8,128)(2,1)}) %all-gather.21.cloned.1.call-update) | async-done | bytes 5767184 | tf_op jit(solution)/shard_map/all_gather | solution.py:279
  1163.1 21.0 %convolution_convert_fusion.1 = bf16[1024,2048]{1,0:T(8,128)(2,1)} fusion(bf16[1408,2048]{1,0:T(8,128)(2,1)} %all-gather.23.cloned.1.call-done, f32[1024,1408]{1,0:T(8,128)} %fusion.53, bf16[2048,1408]{1,0:T(8,128)(2,1)} %all-gather.21.cloned.1.call-done, bf16[1024,2048]{1,0:T(8,128)(2,1)} %all-gather.17.cloned.1.call-done, f32[1024]{0:T(1024)S(1)} %add_rsqrt_fusion.4), kind=kOutput, calls=%fused_computation.107 | convolution fusion | flops 11828199424 | bytes 25694208 | tf_op jit(solution)/shard_map/dot_general | solution.py:283
  1196.3 93.0 %all-gather.13.cloned.1.call-done = bf16[64,65536]{1,0:T(8,128)(2,1)} async-done(((bf16[8,65536]{1,0:T(8,128)(2,1)}), bf16[64,65536]{1,0:T(8,128)(2,1)}) %all-gather.13.cloned.1.call-update) | async-done | bytes 8388624 | tf_op jit(solution)/shard_map/all_gather | solution.py:251
  1295.7 38.9 %reduce-scatter.5.cloned.1.call-done = bf16[1024,512]{1,0:T(8,128)(2,1)} async-done(((bf16[1024,2048]{1,0:T(8,128)(2,1)}), bf16[1024,512]{1,0:T(8,128)(2,1)}) %reduce-scatter.5.cloned.1.call-update) | async-done | bytes 1048592 | tf_op jit(solution)/shard_map/reduce_scatter | solution.py:289
  (485 shorter events, 382.2 us)
Async XLA Ops:
  7.2 169.8 %copy-start = (bf16[2048,4]{0,1:T(4,128)(2,1)S(1)}, bf16[2048,4]{0,1:T(4,128)(2,1)}, u32[]{:S(2)}) copy-start(bf16[2048,4]{0,1:T(4,128)(2,1)} %param.28) | copy-start | bytes 49156
  7.2 109.7 %all-gather.11.cloned.1.call-start = ((), (), s32[]{:S(2)}) async-start(), calls=%async_computation.4 | async-start | bytes 7077888 | tf_op jit(solution)/shard_map/all_gather | solution.py:164
  15.0 158.7 %all-gather.9.cloned.1.call-start = ((), (), s32[]{:S(2)}) async-start(), calls=%async_computation.3 | async-start | bytes 5242880 | tf_op jit(solution)/shard_map/all_gather | solution.py:158
  15.8 107.2 %copy-start.12 = (s32[1,8]{1,0:T(1,128)S(1)}, s32[1,8]{1,0:T(1,128)}, u32[]{:S(2)}) copy-start(s32[1,8]{1,0:T(1,128)} %param.31) | copy-start | bytes 100
  15.8 110.8 %copy-start.8 = (f32[4,1536]{1,0:T(4,128)S(1)}, f32[4,1536]{1,0:T(4,128)}, u32[]{:S(2)}) copy-start(f32[4,1536]{1,0:T(4,128)} %param.27) | copy-start | bytes 73732
  15.8 110.8 %copy-start.9 = (f32[128]{0:T(128)S(1)}, f32[128]{0:T(128)}, u32[]{:S(2)}) copy-start(f32[128]{0:T(128)} %param.30) | copy-start | bytes 1540
  116.9 98.4 %all-to-all-start = ((bf16[512,16,384]{2,0,1:T(8,128)(2,1)}), bf16[512,16,384]{2,0,1:T(8,128)(2,1)}, u32[]{:S(2)}, u32[]{:S(2)}) async-start(bf16[512,16,384]{2,0,1:T(8,128)(2,1)} %all-gather.11.cloned.1.call-done), calls=%async_computation | async-start | bytes 12582912 | tf_op jit(solution)/shard_map/all_to_all | solution.py:165
  122.2 54.8 %copy-start.10 = (f32[2048]{0:T(1024)S(1)}, f32[2048]{0:T(1024)}, u32[]{:S(2)}) copy-start(f32[2048]{0:T(1024)} %param.24) | copy-start | bytes 24580
  122.2 54.8 %copy-start.13 = (f32[4]{0:T(128)S(1)}, f32[4]{0:T(128)}, u32[]{:S(2)}) copy-start(f32[4]{0:T(128)} %param.29) | copy-start | bytes 52
  122.2 670.4 %all-gather.15.cloned.1.call-start = ((), (), s32[]{:S(2)}) async-start(), calls=%async_computation.6 | async-start | bytes 2359296 | tf_op jit(solution)/shard_map/all_gather | solution.py:262
  122.9 720.8 %reduce-scatter.3.cloned.1.call-start = ((), (), s32[]{:S(2)}) async-start(), calls=%async_computation.7 | async-start | bytes 5242880 | tf_op jit(solution)/shard_map/reduce_scatter | solution.py:266
  236.8 4.0 copy-start.6
  288.1 36.9 %collective-permute-start = (bf16[3,1536]{1,0:T(4,128)(2,1)S(1)}, bf16[3,1536]{1,0:T(4,128)(2,1)S(1)}, u32[]{:S(2)}, u32[]{:S(2)}) collective-permute-start(bf16[3,1536]{1,0:T(4,128)(2,1)S(1)} %slice.151), channel_id=1, source_target_pairs={{0,4},{4,8},{8,12},{12,16},{16,20},{20,24},{24,28},{1,5},{5,9},{9,... | collective-permute-start | bytes 27656 | tf_op jit(solution)/shard_map/ppermute | solution.py:17
  292.2 35.2 %collective-permute-start.1 = (bf16[4,128,128]{2,1,0:T(8,128)(2,1)S(1)}, bf16[4,128,128]{2,1,0:T(8,128)(2,1)S(1)}, u32[]{:S(2)}, u32[]{:S(2)}) collective-permute-start(bf16[4,128,128]{2,1,0:T(8,128)(2,1)S(1)} %fusion.74), channel_id=1, source_target_pairs={{0,4},{4,8},{8,12},{12,16},{16,20},{20,24},{24,28},{1,5},{5,9},{9,... | collective-permute-start | bytes 393224 | tf_op jit(solution)/shard_map/ppermute | solution.py:17
  799.4 44.3 %copy-start.4 = (bf16[1024,512]{1,0:T(8,128)(2,1)S(1)}, bf16[1024,512]{1,0:T(8,128)(2,1)}, u32[]{:S(2)}) copy-start(bf16[1024,512]{1,0:T(8,128)(2,1)} %param.23) | copy-start | bytes 3145732
  799.4 49.0 %copy-start.3 = (bf16[16,4,128,128]{3,2,1,0:T(8,128)(2,1)S(1)}, bf16[16,4,128,128]{3,2,1,0:T(8,128)(2,1)}, u32[]{:S(2)}) copy-start(bf16[16,4,128,128]{3,2,1,0:T(8,128)(2,1)} %get-tuple-element.123) | copy-start | bytes 6291460
  799.4 81.4 %all-gather.17.cloned.1.call-start = ((), (), s32[]{:S(2)}) async-start(), calls=%async_computation.8 | async-start | bytes 5242880 | tf_op jit(solution)/shard_map/all_gather | solution.py:270
  846.2 129.6 %all-gather.19.cloned.1.call-start = ((), (), s32[]{:S(2)}) async-start(), calls=%async_computation.9 | async-start | bytes 6488064 | tf_op jit(solution)/shard_map/all_gather | solution.py:274
  846.8 223.1 %all-gather.23.cloned.1.call-start = ((), (), s32[]{:S(2)}) async-start(), calls=%async_computation.11 | async-start | bytes 6488064 | tf_op jit(solution)/shard_map/all_gather | solution.py:285
  847.6 315.6 %all-gather.21.cloned.1.call-start = ((), (), s32[]{:S(2)}) async-start(), calls=%async_computation.10 | async-start | bytes 6488064 | tf_op jit(solution)/shard_map/all_gather | solution.py:279
  848.3 441.1 %all-gather.13.cloned.1.call-start = ((), (), s32[]{:S(2)}) async-start(), calls=%async_computation.5 | async-start | bytes 9437184 | tf_op jit(solution)/shard_map/all_gather | solution.py:251
  850.8 483.8 %reduce-scatter.5.cloned.1.call-start = ((), (), s32[]{:S(2)}) async-start(), calls=%async_computation.12 | async-start | bytes 5242880 | tf_op jit(solution)/shard_map/reduce_scatter | solution.py:289
  1289.4 47.7 %copy-start.1 = (bf16[2048,4]{0,1:T(4,128)(2,1)S(1)}, bf16[2048,4]{0,1:T(4,128)(2,1)}, u32[]{:S(2)}) copy-start(bf16[2048,4]{0,1:T(4,128)(2,1)} %param.28) | copy-start | bytes 49156
  1294.0 40.6 %copy-start.2 = (bf16[1024,512]{1,0:T(8,128)(2,1)S(1)}, bf16[1024,512]{1,0:T(8,128)(2,1)}, u32[]{:S(2)}) copy-start(bf16[1024,512]{1,0:T(8,128)(2,1)} %add_convert_fusion.1) | copy-start | bytes 3145732
  (5 other events, 10.2 us)
Sparse Core Ops, SparseCore 0:
  15.2 101.7 all-gather.10
  118.5 55.1 all-gather.8
  175.7 50.8 all-gather.14
  799.5 44.1 reduce-scatter.2
  846.3 34.4 all-gather.16
  883.1 92.6 all-gather.18
  978.1 91.7 all-gather.22
  1072.3 90.8 all-gather.20
  1166.1 123.2 all-gather.12
  1291.9 42.6 reduce-scatter.4
where the time goes:
time: 1350 us; the launch traced here: 1340 us
  waiting for transfers between devices  657 us (49%)
  other arithmetic  394 us (29%)
  matrix products  109 us (8%)
  local copies, waits for them, and re-layouts  74.3 us (6%)
  loops' own time  42.5 us (3%)
  starting transfers between devices  41.1 us (3%)
  between operations  16.2 us (1%)
    another operation x16, other arithmetic, span_step(): lax.linalg.triangular_solve(system, solve_target_vector, left_side=True,...  315 us
    all_gather x1, waiting for transfers between devices, shards(): trainer_rows = lax.all_gather(ordered, 'group', axis=0, tiled=True)  101 us
    all_gather x1, waiting for transfers between devices, shards(): lax.all_gather(up_weight, 'group', axis=0, tiled=True)  93.3 us
    all_gather x1, waiting for transfers between devices, shards(): lax.all_gather(finals.astype(jnp.bfloat16), 'group', axis=0, tiled=True)  93 us
    all_gather x1, waiting for transfers between devices, shards(): lax.all_gather(gate_weight, 'group', axis=0, tiled=True)  91.9 us
    all_gather x1, waiting for transfers between devices, shards(): lax.all_gather(down_weight, 'group', axis=1, tiled=True)  82.1 us
    reduce_scatter x1, waiting for transfers between devices, shards(): lax.psum_scatter(mixer_terms.astype(jnp.bfloat16), 'mp', scatter_dimensio...  44.2 us
    all_gather x1, waiting for transfers between devices, shards(): gathered = lax.all_gather(tokens, 'mp', axis=1, tiled=True)  41.9 us
  transfers between devices with their start and end apart: 13, of which 11 were waited for; matrix products, arithmetic and copies ran while one was open for 41% of the time, Pallas kernels for 0%

commit v1 on v0

v1 whole, which is shorter than its diff:
```python
from functools import partial

import jax
import jax.numpy as jnp
from jax import lax
from jax.experimental import pallas as pl
from jax.experimental.pallas import tpu as pltpu
from jax.sharding import PartitionSpec as P

SPAN = 64
EPSILON = 1e-06
F32 = jnp.float32
BF16 = jnp.bfloat16
MIB = 1 << 20


def from_behind(value, axis, steps):
    count = lax.axis_size(axis)
    initial, last = (max(0, -steps), min(count, count - steps))
    return lax.ppermute(value, axis, [(source, source + steps) for source in range(initial, last)])


def normalize_rows(matrix, scaling):
    widened = matrix.astype(F32)
    return (
        widened * lax.rsqrt(jnp.mean(widened * widened, axis=-1, keepdims=True) + EPSILON) * scaling
    )


def mm(a, b):
    return lax.dot_general(a, b, (((1,), (0,)), ((), ())), preferred_element_type=F32)


def mm_nt(a, b):
    return lax.dot_general(a, b, (((1,), (1,)), ((), ())), preferred_element_type=F32)


def mm_tn(a, b):
    return lax.dot_general(a, b, (((0,), (0,)), ((), ())), preferred_element_type=F32)


def two(x):
    high = x.astype(BF16)
    return high, (x - high.astype(F32)).astype(BF16)


def mm3(a, b, product=mm):
    return product(a[0], b[0]) + (product(a[0], b[1]) + product(a[1], b[0]))


def order_kernel(slot_ref, x_ref, o_ref):
    o_ref[0] = x_ref[...].astype(BF16)


def order_heads(trainer, slot_of_head, parts, heads, joined):
    rows = trainer.shape[0]
    per = heads // parts
    return pl.pallas_call(
        order_kernel,
        grid_spec=pltpu.PrefetchScalarGridSpec(
            num_scalar_prefetch=1,
            grid=(heads,),
            in_specs=[pl.BlockSpec((rows, joined), lambda h, s: (0, s[h]))],
            out_specs=pl.BlockSpec((1, rows, joined), lambda h, s: (h // per, 0, h % per)),
        ),
        out_shape=jax.ShapeDtypeStruct((parts, rows, per * joined), BF16),
        name="order_heads",
    )(slot_of_head, trainer)


def intra_one(flag, before, rows, taps, gating, heads, dk):
    count = rows.shape[0]
    lead = before.shape[0]
    history = jnp.where(flag, 0.0, before.astype(F32))
    extended = jnp.concatenate([history, rows.astype(F32)], axis=0)
    mixed = extended[lead:] * taps[0:1]
    for lag in range(1, taps.shape[0]):
        mixed = mixed + pltpu.roll(extended, lag, 0)[lead:] * taps[lag : lag + 1]
    active = mixed * jax.nn.sigmoid(mixed)

    def stacked(part):
        return jnp.concatenate(
            [active[:, (3 * h + part) * dk : (3 * h + part + 1) * dk] for h in range(heads)], axis=0
        )

    query, key, value = stacked(0), stacked(1), stacked(2)
    query = query * (
        lax.rsqrt(jnp.sum(query * query, axis=-1, keepdims=True) + EPSILON) * dk ** (-0.5)
    )
    key = key * lax.rsqrt(jnp.sum(key * key, axis=-1, keepdims=True) + EPSILON)
    beta = jnp.concatenate([gating[:, h : h + 1] for h in range(heads)], axis=0)

    size = heads * count
    row = lax.broadcasted_iota(jnp.int32, (size, size), 0)
    col = lax.broadcasted_iota(jnp.int32, (size, size), 1)
    far = row ^ col
    same = (far < count) & (row >= col)
    keys = two(key)
    gram = mm3(keys, keys, mm_nt)
    lower = jnp.where(same & (row > col), beta * gram, 0.0)
    inverse = jnp.where(row == col, 1.0, 0.0) - jnp.where(far == 1, lower, 0.0)
    step = 2
    while step < count:
        corner = two(jnp.where((far >= step) & (far < 2 * step), lower, 0.0))
        halves = two(inverse)
        inverse = inverse - mm3(halves, two(mm3(corner, halves)))
        step *= 2
    target = jnp.concatenate([key * beta, value * beta], axis=1)
    solved = mm3(two(inverse), two(target)).astype(BF16)
    query16 = query.astype(BF16)
    scores = jnp.where(same, mm_nt(query16, keys[0]), 0.0).astype(BF16)
    mixed_in = mm(scores, solved)
    out_query = (query - mixed_in[:, :dk]).astype(BF16)
    out_base = mixed_in[:, dk:]
    moves = [
        mm_tn(keys[0][h * count : (h + 1) * count], solved[h * count : (h + 1) * count])
        for h in range(heads)
    ]
    return out_query, out_base, moves


def intra_kernel(per, heads, dk, flags, first_ref, before_ref, rows_ref, taps_ref, gate_ref,
                 query_ref, base_ref, decay_ref, add_ref):
    step = pl.program_id(0)
    taps = taps_ref[...]
    for j in range(per):
        if j == 0:
            before = jnp.where(step == 0, first_ref[...], before_ref[...])
        else:
            before = rows_ref[j * SPAN - 16 : j * SPAN]
        out_query, out_base, moves = intra_one(
            flags[step * per + j] > 0, before, rows_ref[j * SPAN : (j + 1) * SPAN], taps,
            gate_ref[j * SPAN : (j + 1) * SPAN], heads, dk,
        )
        query_ref[j] = out_query
        base_ref[j] = out_base
        for h in range(heads):
            decay_ref[j, h] = moves[h][:, :dk].astype(BF16)
            add_ref[j, h] = moves[h][:, dk:]


def intra(flags, first, projected, taps, gating, heads, dk, per=2):
    total, width = projected.shape
    spans = total // SPAN
    size = heads * SPAN
    grid = spans // per
    ahead = per * SPAN // 16
    return pl.pallas_call(
        partial(intra_kernel, per, heads, dk),
        grid_spec=pltpu.PrefetchScalarGridSpec(
            num_scalar_prefetch=1,
            grid=(grid,),
            in_specs=[
                pl.BlockSpec((16, width), lambda i, f: (0, 0)),
                pl.BlockSpec((16, width), lambda i, f: (jnp.maximum(i * ahead - 1, 0), 0)),
                pl.BlockSpec((per * SPAN, width), lambda i, f: (i, 0)),
                pl.BlockSpec(taps.shape, lambda i, f: (0, 0)),
                pl.BlockSpec((per * SPAN, heads), lambda i, f: (i, 0)),
            ],
            out_specs=[
                pl.BlockSpec((per, size, dk), lambda i, f: (i, 0, 0)),
                pl.BlockSpec((per, size, dk), lambda i, f: (i, 0, 0)),
                pl.BlockSpec((per, heads, dk, dk), lambda i, f: (i, 0, 0, 0)),
                pl.BlockSpec((per, heads, dk, dk), lambda i, f: (i, 0, 0, 0)),
            ],
        ),
        out_shape=[
            jax.ShapeDtypeStruct((spans, size, dk), BF16),
            jax.ShapeDtypeStruct((spans, size, dk), F32),
            jax.ShapeDtypeStruct((spans, heads, dk, dk), BF16),
            jax.ShapeDtypeStruct((spans, heads, dk, dk), F32),
        ],
        compiler_params=pltpu.CompilerParams(vmem_limit_bytes=40 * MIB),
        cost_estimate=pl.CostEstimate(
            flops=60_000_000_000, bytes_accessed=200_000_000, transcendentals=0
        ),
        name="intra",
    )(flags, first, projected, projected, taps, gating)


def tail_kernel(heads, start, decay_ref, add_ref, prior_ref, out_ref, memory):
    memory[...] = prior_ref[0]

    def body(i, carry):
        for h in range(heads):
            old = memory[h]
            memory[h] = old + add_ref[i, h] - mm(decay_ref[i, h], old.astype(BF16))
        return carry

    lax.fori_loop(start[0], decay_ref.shape[0], body, 0)
    out_ref[...] = memory[...].astype(BF16)


def tail(start, decay, add, prior):
    spans, heads, dk, _ = decay.shape
    slots = prior.shape[0]
    return pl.pallas_call(
        partial(tail_kernel, heads),
        grid_spec=pltpu.PrefetchScalarGridSpec(
            num_scalar_prefetch=1,
            grid=(1,),
            in_specs=[
                pl.BlockSpec(decay.shape, lambda i, s: (0, 0, 0, 0)),
                pl.BlockSpec(add.shape, lambda i, s: (0, 0, 0, 0)),
                pl.BlockSpec((1, heads, dk, dk), lambda i, s: (slots - 1, 0, 0, 0)),
            ],
            out_specs=pl.BlockSpec((heads, dk, dk), lambda i, s: (0, 0, 0)),
            scratch_shapes=[pltpu.VMEM((heads, dk, dk), F32)],
        ),
        out_shape=jax.ShapeDtypeStruct((heads, dk, dk), BF16),
        compiler_params=pltpu.CompilerParams(vmem_limit_bytes=40 * MIB),
        name="tail",
    )(start, decay, add, prior)


def scan_kernel(heads, dk, seg, starts, dest, linked, decay_ref, add_ref, query_ref, base_ref,
                prior_ref, handed_ref, gain_ref, out_ref, send_ref, memory):
    i = pl.program_id(0)

    @pl.when(starts[i] > 0)
    def _():
        memory[...] = prior_ref[0]

    @pl.when((i == 0) & (linked[0] > 0))
    def _():
        memory[...] = handed_ref[...].astype(F32)

    for h in range(heads):
        old = memory[h]
        old16 = old.astype(BF16)
        at = slice(h * SPAN, (h + 1) * SPAN)
        rows = mm(query_ref[0, at], old16) + base_ref[0, at]
        rows = rows * lax.rsqrt(jnp.mean(rows * rows, axis=-1, keepdims=True) + EPSILON)
        out_ref[:, h * dk : (h + 1) * dk] = (rows * gain_ref[...]).astype(BF16)
        new = old + add_ref[0, h] - mm(decay_ref[0, h], old16)
        memory[h] = new
        send_ref[0, h] = new.astype(BF16)


def scan(seg, starts, dest, linked, decay, add, query, base, prior, handed, gain, slots):
    spans, heads, dk, _ = decay.shape
    size = heads * SPAN
    return pl.pallas_call(
        partial(scan_kernel, heads, dk),
        grid_spec=pltpu.PrefetchScalarGridSpec(
            num_scalar_prefetch=4,
            grid=(spans,),
            in_specs=[
                pl.BlockSpec((1, heads, dk, dk), lambda i, g, s, d, k: (i, 0, 0, 0)),
                pl.BlockSpec((1, heads, dk, dk), lambda i, g, s, d, k: (i, 0, 0, 0)),
                pl.BlockSpec((1, size, dk), lambda i, g, s, d, k: (i, 0, 0)),
                pl.BlockSpec((1, size, dk), lambda i, g, s, d, k: (i, 0, 0)),
                pl.BlockSpec((1, heads, dk, dk), lambda i, g, s, d, k: (g[i], 0, 0, 0)),
                pl.BlockSpec((heads, dk, dk), lambda i, g, s, d, k: (0, 0, 0)),
                pl.BlockSpec((1, dk), lambda i, g, s, d, k: (0, 0)),
            ],
            out_specs=[
                pl.BlockSpec((SPAN, heads * dk), lambda i, g, s, d, k: (i, 0)),
                pl.BlockSpec((1, heads, dk, dk), lambda i, g, s, d, k: (d[i], 0, 0, 0)),
            ],
            scratch_shapes=[pltpu.VMEM((heads, dk, dk), F32)],
        ),
        out_shape=[
            jax.ShapeDtypeStruct((spans * SPAN, heads * dk), BF16),
            jax.ShapeDtypeStruct((slots, heads, dk, dk), BF16),
        ],
        compiler_params=pltpu.CompilerParams(vmem_limit_bytes=40 * MIB),
        cost_estimate=pl.CostEstimate(
            flops=10_000_000_000, bytes_accessed=40_000_000, transcendentals=0
        ),
        name="scan",
    )(seg, starts, dest, linked, decay, add, query, base, prior, handed, gain)


def place_kernel(index, x_ref, o_ref):
    o_ref[...] = x_ref[...].astype(F32)


def place(index, got, count):
    _, heads, dk, _ = got.shape
    return pl.pallas_call(
        place_kernel,
        grid_spec=pltpu.PrefetchScalarGridSpec(
            num_scalar_prefetch=1,
            grid=(count,),
            in_specs=[pl.BlockSpec((1, heads, dk, dk), lambda p, s: (s[p], 0, 0, 0))],
            out_specs=pl.BlockSpec((1, heads, dk, dk), lambda p, s: (p, 0, 0, 0)),
        ),
        out_shape=jax.ShapeDtypeStruct((count, heads, dk, dk), F32),
        name="place",
    )(index, got)


CAP = 2


def page_plan(page_table, requests):
    me = lax.axis_index("group")
    groups = lax.axis_size("group")
    tables = lax.all_gather(page_table, "group", axis=0, tiled=True).reshape(groups, requests)
    owner = tables // requests
    earlier = jnp.tril(jnp.ones((requests, requests), jnp.int32), -1)
    rank = jnp.sum((owner[:, :, None] == owner[:, None, :]) * earlier[None], axis=2)
    mine = jnp.arange(groups, dtype=jnp.int32) == me
    outgoing = jnp.sum(jnp.where(mine[:, None], owner * CAP + rank, 0), axis=0)
    wanted = me * requests + jnp.arange(requests, dtype=jnp.int32)
    sources = jnp.arange(groups, dtype=jnp.int32)[:, None] * CAP + rank
    hit = tables[:, :, None] == wanted[None, None, :]
    incoming = jnp.sum(jnp.where(hit, sources[:, :, None], 0), axis=(0, 1))
    return outgoing.astype(jnp.int32), incoming.astype(jnp.int32)


def shards(
    tokens,
    in_gain,
    trainer_qkv,
    head_order,
    conv_weight,
    beta_weight,
    beta_bias,
    out_gain,
    lengths,
    prior_states,
    page_table,
    o_weight,
    gate_weight,
    up_weight,
    down_weight,
):
    mp_count = lax.axis_size("mp")
    group_count = lax.axis_size("group")
    head_total = head_order.shape[0]
    local_heads = head_total // mp_count
    dk = prior_states.shape[2]
    requests = prior_states.shape[0]
    joined_width = 3 * dk
    gathered = lax.all_gather(tokens, "mp", axis=1, tiled=True)
    token_total = gathered.shape[0]
    spans = token_total // SPAN
    heads_of = jnp.arange(head_total, dtype=jnp.int32)
    slot_of_head = jnp.sum(
        jnp.where(head_order[None, :] == heads_of[:, None], heads_of[None, :], 0), axis=1
    ).astype(jnp.int32)
    ordered = order_heads(trainer_qkv, slot_of_head, mp_count, head_total, joined_width)
    shared = lax.all_to_all(ordered, "mp", split_axis=0, concat_axis=0)
    arranged = lax.all_gather(
        shared.reshape(-1, local_heads * joined_width), "group", axis=0, tiled=True
    )
    normed = normalize_rows(gathered, in_gain).astype(BF16)
    gating_all = jax.nn.sigmoid(
        jnp.dot(normed, beta_weight, preferred_element_type=F32) + beta_bias
    )
    projected = jnp.dot(normed, arranged, preferred_element_type=F32).astype(BF16)

    row = lengths[0].astype(jnp.int32)
    order = jnp.arange(requests, dtype=jnp.int32)
    starts = jnp.sum(jnp.where(order[None, :] < order[:, None], row[None, :], 0), axis=1)
    span_ids = jnp.arange(spans, dtype=jnp.int32)
    seg_of_span = jnp.sum((span_ids[:, None] >= starts[None, :]).astype(jnp.int32), axis=1) - 1
    is_start = jnp.any(span_ids[:, None] == starts[None, :], axis=1).astype(jnp.int32)
    linked = (lax.axis_index("group") > 0).astype(jnp.int32)
    begins = is_start * jnp.where(span_ids == 0, 1 - linked, 1)
    outgoing, incoming = page_plan(page_table, requests)
    dest = jnp.sum(
        jnp.where(seg_of_span[:, None] == order[None, :], outgoing[None, :], 0), axis=1
    ).astype(jnp.int32)

    behind = from_behind(projected[token_total - 16 :], "group", 1)
    query, base, decay, add = intra(
        begins, behind, projected, conv_weight, gating_all, local_heads, dk
    )
    last = tail(starts[-1:].astype(jnp.int32), decay, add, prior_states)
    handed = from_behind(last, "group", 1)
    attended, leaving = scan(
        seg_of_span.astype(jnp.int32), is_start, dest, linked[None], decay, add, query, base,
        prior_states, handed, out_gain[None], group_count * CAP,
    )
    arrived = lax.all_to_all(leaving, "group", split_axis=0, concat_axis=0, tiled=True)
    state_pages = place(incoming, arrived, requests)

    mixer_terms = jnp.dot(
        attended,
        lax.all_gather(o_weight, "group", axis=1, tiled=True),
        preferred_element_type=F32,
    ).astype(BF16)
    mixer_sum = lax.psum_scatter(mixer_terms, "mp", scatter_dimension=1, tiled=True).astype(F32)
    residual_one = (tokens.astype(F32) + mixer_sum).astype(BF16)
    mixed_rows = lax.all_gather(residual_one, "mp", axis=1, tiled=True)
    post_normed = normalize_rows(mixed_rows, 1.0).astype(BF16)
    gate_part = jnp.dot(
        post_normed,
        lax.all_gather(gate_weight, "group", axis=0, tiled=True),
        preferred_element_type=F32,
    )
    up_part = jnp.dot(
        post_normed,
        lax.all_gather(up_weight, "group", axis=0, tiled=True),
        preferred_element_type=F32,
    )
    hidden = (jax.nn.silu(gate_part) * up_part).astype(BF16)
    feed_terms = jnp.dot(
        hidden,
        lax.all_gather(down_weight, "group", axis=1, tiled=True),
        preferred_element_type=F32,
    ).astype(BF16)
    feed_sum = lax.psum_scatter(feed_terms, "mp", scatter_dimension=1, tiled=True).astype(F32)
    layer_out = (residual_one.astype(F32) + feed_sum).astype(BF16)
    return (attended, state_pages, layer_out)


def solution(mesh):
    in_specs = (
        P("group", "mp"),
        P(),
        P(("group", "mp"), None),
        P(),
        P(None, "mp"),
        P(None, "mp"),
        P("mp"),
        P(),
        P("group", None),
        P("group", "mp", None, None),
        P("group"),
        P("mp", "group"),
        P("group", "mp"),
        P("group", "mp"),
        P("mp", "group"),
    )
    out_specs = (P("group", "mp"), P("group", "mp", None, None), P("group", "mp"))
    return jax.shard_map(shards, mesh=mesh, in_specs=in_specs, out_specs=out_specs, check_vma=False)
```

time: 1350 us -> 718 us (0.53)
  other arithmetic: 394 us -> 13.9 us
  waiting for transfers between devices: 657 us -> 494 us
  Pallas kernels: 0 us -> 91.3 us
  local copies, waits for them, and re-layouts: 74.3 us -> 2.91 us
  matrix products: 109 us -> 51.1 us
  loops' own time: 42.5 us -> 0 us
  starting transfers between devices: 41.1 us -> 11 us
  blocking collectives: 10.1 us -> 37.7 us
    another operation x17 -> x0, other arithmetic: 315 us -> none  [the longest x16 315 us: span_step(): lax.linalg.triangular_solve(system, solve_target_vector, left_side=True,...]
    all_gather x2 -> x1, waiting for transfers between devices: 194 us -> 92.7 us  [shards(): lax.all_gather(shared.reshape(-1, local_heads * joined_width), 'group', a...]
    pallas_call x0 -> x5, Pallas kernels: none -> 91.3 us  [the longest x1 66 us: intra(): pl.pallas_call(partial(intra_kernel, per, heads, dk), grid_spec=pltpu.Pre...]
    dot_general x99 -> x2, matrix products: 62.3 us -> 12 us  [the longest x1 10.7 us: shards(): jnp.dot(normed, arranged, preferred_element_type=F32).astype(BF16)]
    another operation x2 -> x0, loops' own time: 42.5 us -> none  [the longest x1 40.5 us: shards(): lax.fori_loop(jnp.int32(0), last_start, partial(advance, initial=initial,...]
    all_gather x1, waiting for transfers between devices: 41.9 us -> 0.01 us  [shards(): gathered = lax.all_gather(tokens, 'mp', axis=1, tiled=True)]
    reduce_scatter x2, waiting for transfers between devices: 83.1 us -> 48.8 us  [the longest x1 48.8 us: shards(): lax.psum_scatter(mixer_terms, 'mp', scatter_dimension=1, tiled=True)]
    ppermute x2, starting transfers between devices: 35.2 us -> 6.9 us  [from_behind(): lax.ppermute(value, axis, [(source, source + steps) for source in range(i...]
  transfers between devices with their start and end apart: 13 -> 12, of which waited for: 11 -> 9; matrix products, arithmetic and copies ran while one was open for 41% -> 5% of each run, Pallas kernels for 0% -> 13%
where the time goes in v1:
time: 718 us; the launch traced here: 717 us
  waiting for transfers between devices  494 us (69%)
  Pallas kernels  91.3 us (13%)
  matrix products  51.1 us (7%)
  blocking collectives  37.7 us (5%)
  between operations  14.8 us (2%)
  other arithmetic  13.9 us (2%)
  starting transfers between devices  11 us (2%)
    all_gather x1, waiting for transfers between devices, shards(): lax.all_gather(up_weight, 'group', axis=0, tiled=True)  93.3 us
    all_gather x1, waiting for transfers between devices, shards(): lax.all_gather(shared.reshape(-1, local_heads * joined_width), 'group', a...  92.7 us
    all_gather x1, waiting for transfers between devices, shards(): lax.all_gather(gate_weight, 'group', axis=0, tiled=True)  91.9 us
    all_gather x1, waiting for transfers between devices, shards(): lax.all_gather(down_weight, 'group', axis=1, tiled=True)  82.2 us
    pallas_call x1, Pallas kernels, intra(): pl.pallas_call(partial(intra_kernel, per, heads, dk), grid_spec=pltpu.Pre...  66 us
    reduce_scatter x1, waiting for transfers between devices, shards(): lax.psum_scatter(mixer_terms, 'mp', scatter_dimension=1, tiled=True)  48.8 us
    all_to_all x1, waiting for transfers between devices, shards(): lax.all_to_all(leaving, 'group', split_axis=0, concat_axis=0, tiled=True)  47.1 us
    all_gather x1, waiting for transfers between devices, shards(): mixed_rows = lax.all_gather(residual_one, 'mp', axis=1, tiled=True)  32.5 us
  transfers between devices with their start and end apart: 12, of which 9 were waited for; matrix products, arithmetic and copies ran while one was open for 5% of the time, Pallas kernels for 13%

profile of v1, /device:TPU:0, one launch (start us, length us, event | category | flops | bytes accessed | tf_op | source)
XLA Modules:
  0.0 717.1 jit_solution(16322821575865275144)
XLA Ops:
  9.3 9.9 %order_heads.1 = bf16[4,64,1536]{2,1,0:T(8,128)(2,1)} custom-call(s32[16]{0:T(128)} %select_reduce_fusion.2.slot_ref, f32[64,6144]{1,0:T(8,128)} %x_ref.1), custom_call_target="tpu_custom_call" | custom-call | tf_op jit(solution)/shard_map/order_heads/pallas_call | solution.py:58
  19.1 25.5 %all_to_all.10 = bf16[4,64,1536]{2,1,0:T(8,128)(2,1)} all-to-all(bf16[4,64,1536]{2,1,0:T(8,128)(2,1)} %order_heads.1), channel_id=1, replica_groups=mesh['group'=8,'mp'=4] {'mp'}, dimensions={0} | all-to-all | bytes 1572864 | tf_op jit(solution)/shard_map/all_to_all | solution.py:345
  48.0 12.2 %all-reduce = s32[64]{0:T(128)S(1)} all-reduce(s32[64]{0:T(128)S(1)} %dynamic-update-slice), channel_id=1, replica_groups=mesh['group'=8,'mp'=4] {'group'}, use_global_device_ids=true, to_apply=%add | all-reduce | flops 64 | bytes 512
  60.7 3.1 fusion
  63.8 92.7 %all-gather.10.cloned.1.call-done = bf16[2048,1536]{1,0:T(8,128)(2,1)} async-done(((bf16[256,1536]{1,0:T(8,128)(2,1)}), bf16[2048,1536]{1,0:T(8,128)(2,1)}) %all-gather.10.cloned.1.call-update) | async-done | bytes 6291472 | tf_op jit(solution)/shard_map/all_gather | solution.py:346
  156.5 10.7 %convolution_convert_fusion.before_ref.rows_ref = bf16[1024,1536]{1,0:T(8,128)(2,1)S(1)} fusion(bf16[2048,1536]{1,0:T(8,128)(2,1)} %all-gather.10.cloned.1.call-done, bf16[1024,2048]{1,0:T(8,128)(2,1)} %all-gather.8.cloned.1.call-done, f32[2048]{0:T(1024)S(1)} %copy-done.9, f32[1024]{0:T(1024)S(1)} %add_rsqrt_fusion.1), kind=kOutput, calls=%fused_computation.10 | convolution fusion | flops 6452412416 | bytes 13643776 | tf_op jit(solution)/shard_map/dot_general | solution.py:353
  167.2 2.5 collective-permute-start
  171.4 66.0 %intra.1 = (bf16[16,256,128]{2,1,0:T(8,128)(2,1)S(1)}, f32[16,256,128]{2,1,0:T(8,128)S(1)}, bf16[16,4,128,128]{3,2,1,0:T(8,128)(2,1)S(1)}, f32[16,4,128,128]{3,2,1,0:T(8,128)S(1)}) custom-call(s32[16]{0:T(128)S(1)} %fusion.18.flags, bf16[16,1536]{1,0:T(8,128)(2,1)S(1)} %collective-permute-done.first_ref, ...), custom_call_target="tpu_custom_call" | custom-call | flops 60000002048 | bytes 200000000 | tf_op jit(solution)/shard_map/intra/pallas_call | solution.py:148
  238.3 4.4 collective-permute-start.1
  245.1 8.5 %scan.1 = (bf16[1024,512]{1,0:T(8,128)(2,1)}, bf16[16,4,128,128]{3,2,1,0:T(8,128)(2,1)}) custom-call(s32[16]{0:T(128)S(1)} %broadcast_add_fusion.1.seg, s32[16]{0:T(128)S(1)} %convert_element_type.53.starts, s32[16]{0:T(128)S(1)} %select_reduce_fusion.3.dest, s32[1]{0:T(128)} %bitcast.2.linked, bf16[16,4,128,128]{3,2,1,0:T(8,128)(2,1)S(1)} %get-tuple-element.9.decay_ref, ...), custom_call_target="tpu_custom_call" | custom-call | flops 10000000000 | bytes 40000000 | tf_op jit(solution)/shard_map/scan/pallas_call | solution.py:243
  253.6 6.3 convolution_convert_fusion.2
  259.9 48.8 %reduce-scatter.3.cloned.1.call-done = bf16[1024,512]{1,0:T(8,128)(2,1)} async-done(((bf16[1024,2048]{1,0:T(8,128)(2,1)}), bf16[1024,512]{1,0:T(8,128)(2,1)}) %reduce-scatter.3.cloned.1.call-update) | async-done | bytes 1048592 | tf_op jit(solution)/shard_map/reduce_scatter | solution.py:386
  308.7 2.5 add_convert_fusion.1
  313.4 32.5 %all-gather.14.cloned.1.call-done = bf16[1024,2048]{1,0:T(8,128)(2,1)} async-done(((bf16[1024,512]{1,0:T(8,128)(2,1)}), bf16[1024,2048]{1,0:T(8,128)(2,1)}) %all-gather.14.cloned.1.call-update) | async-done | bytes 4194320 | tf_op jit(solution)/shard_map/all_gather | solution.py:388
  345.9 3.1 fusion.3
  349.0 91.9 %all-gather.16.cloned.1.call-done = bf16[2048,1408]{1,0:T(8,128)(2,1)} async-done(((bf16[256,1408]{1,0:T(8,128)(2,1)}), bf16[2048,1408]{1,0:T(8,128)(2,1)}) %all-gather.16.cloned.1.call-update) | async-done | bytes 5767184 | tf_op jit(solution)/shard_map/all_gather | solution.py:392
  440.8 11.9 %fusion.6 = f32[1024,1408]{1,0:T(8,128)} fusion(bf16[2048,1408]{1,0:T(8,128)(2,1)} %all-gather.16.cloned.1.call-done, bf16[1024,2048]{1,0:T(8,128)(2,1)} %all-gather.14.cloned.1.call-done, f32[1024]{0:T(1024)S(1)} %add_rsqrt_fusion), kind=kOutput, calls=%fused_computation.15 | convolution fusion | flops 5911871488 | bytes 15732736 | tf_op jit(solution)/shard_map/dot_general | solution.py:390
  452.7 82.2 %all-gather.20.cloned.1.call-done = bf16[1408,2048]{1,0:T(8,128)(2,1)} async-done(((bf16[1408,256]{1,0:T(8,128)(2,1)}), bf16[1408,2048]{1,0:T(8,128)(2,1)}) %all-gather.20.cloned.1.call-update) | async-done | bytes 5767184 | tf_op jit(solution)/shard_map/all_gather | solution.py:403
  534.9 93.3 %all-gather.18.cloned.1.call-done = bf16[2048,1408]{1,0:T(8,128)(2,1)} async-done(((bf16[256,1408]{1,0:T(8,128)(2,1)}), bf16[2048,1408]{1,0:T(8,128)(2,1)}) %all-gather.18.cloned.1.call-update) | async-done | bytes 5767184 | tf_op jit(solution)/shard_map/all_gather | solution.py:397
  628.1 20.9 %convolution_convert_fusion.1 = bf16[1024,2048]{1,0:T(8,128)(2,1)} fusion(bf16[1408,2048]{1,0:T(8,128)(2,1)} %all-gather.20.cloned.1.call-done, f32[1024,1408]{1,0:T(8,128)} %fusion.6, bf16[2048,1408]{1,0:T(8,128)(2,1)} %all-gather.18.cloned.1.call-done, bf16[1024,2048]{1,0:T(8,128)(2,1)} %all-gather.14.cloned.1.call-done, f32[1024]{0:T(1024)S(1)} %add_rsqrt_fusion), kind=kOutput, calls=%fused_computation.11 | convolution fusion | flops 11828199424 | bytes 25694208 | tf_op jit(solution)/shard_map/dot_general | solution.py:401
  649.1 3.7 all-to-all-start.1
  653.5 47.1 %all-to-all-done.1.x_ref = bf16[16,4,128,128]{3,2,1,0:T(8,128)(2,1)S(1)} async-done(((bf16[16,4,128,128]{3,2,1,0:T(8,128)(2,1)}), bf16[16,4,128,128]{3,2,1,0:T(8,128)(2,1)S(1)}, u32[]{:S(2)}, u32[]{:S(2)}) %all-to-all-start.1) | async-done | bytes 2097184 | tf_op jit(solution)/shard_map/all_to_all | solution.py:378
  701.9 6.1 place.1
  708.1 2.5 add_convert_fusion
  (78 shorter events, 14.2 us)
Async XLA Ops:
  7.2 162.5 %copy-start = (bf16[2048,4]{0,1:T(4,128)(2,1)S(1)}, bf16[2048,4]{0,1:T(4,128)(2,1)}, u32[]{:S(2)}) copy-start(bf16[2048,4]{0,1:T(4,128)(2,1)} %param.20) | copy-start | bytes 49156
  7.2 39.3 %copy-start.13 = (u32[32]{0:T(128)S(1)}, u32[32]{0:T(128)}, u32[]{:S(2)}) copy-start(u32[32]{0:T(128)} %constant.55) | copy-start | bytes 388
  7.2 38.3 %copy-start.10 = (s32[1,8]{1,0:T(1,128)S(1)}, s32[1,8]{1,0:T(1,128)}, u32[]{:S(2)}) copy-start(s32[1,8]{1,0:T(1,128)} %param.23) | copy-start | bytes 100
  7.2 40.5 %copy-start.11 = (s32[8]{0:T(128)S(1)}, s32[8]{0:T(128)}, u32[]{:S(2)}) copy-start(s32[8]{0:T(128)} %param.25) | copy-start | bytes 100
  7.2 149.3 %copy-start.9 = (f32[2048]{0:T(1024)S(1)}, f32[2048]{0:T(1024)}, u32[]{:S(2)}) copy-start(f32[2048]{0:T(1024)} %param.16) | copy-start | bytes 24580
  7.2 53.4 %all-gather.8.cloned.1.call-start = ((), (), s32[]{:S(2)}) async-start(), calls=%async_computation.4 | async-start | bytes 5242880 | tf_op jit(solution)/shard_map/all_gather | solution.py:337
  8.0 148.5 %all-gather.10.cloned.1.call-start = ((), (), s32[]{:S(2)}) async-start(), calls=%async_computation.5 | async-start | bytes 7077888 | tf_op jit(solution)/shard_map/all_gather | solution.py:346
  44.7 208.9 %all-gather.12.cloned.1.call-start = ((), (), s32[]{:S(2)}) async-start(), calls=%async_computation.6 | async-start | bytes 2359296 | tf_op jit(solution)/shard_map/all_gather | solution.py:383
  45.5 263.3 %reduce-scatter.3.cloned.1.call-start = ((), (), s32[]{:S(2)}) async-start(), calls=%async_computation.7 | async-start | bytes 5242880 | tf_op jit(solution)/shard_map/reduce_scatter | solution.py:386
  63.7 105.9 %copy-start.12 = (f32[4]{0:T(128)S(1)}, f32[4]{0:T(128)}, u32[]{:S(2)}) copy-start(f32[4]{0:T(128)} %param.21) | copy-start | bytes 52
  156.5 13.2 %copy-start.8 = (bf16[1024,2048]{1,0:T(8,128)(2,1)S(1)}, bf16[1024,2048]{1,0:T(8,128)(2,1)}, u32[]{:S(2)}) copy-start(bf16[1024,2048]{1,0:T(8,128)(2,1)} %all-gather.8.cloned.1.call-done) | copy-start | bytes 12582916
  167.2 4.2 collective-permute-start
  171.1 66.4 %copy-start.2 = (f32[8,4,128,128]{3,2,1,0:T(8,128)S(1)}, f32[8,4,128,128]{3,2,1,0:T(8,128)}, u32[]{:S(2)}) copy-start(f32[8,4,128,128]{3,2,1,0:T(8,128)} %prior_ref.3) | copy-start | bytes 6291460
  237.5 7.6 %copy-start.4 = (f32[128]{0:T(128)S(1)}, f32[128]{0:T(128)}, u32[]{:S(2)}) copy-start(f32[128]{0:T(128)} %param.22) | copy-start | bytes 1540
  238.3 6.8 collective-permute-start.1
  253.6 55.1 %copy-start.7 = (bf16[1024,512]{1,0:T(8,128)(2,1)S(1)}, bf16[1024,512]{1,0:T(8,128)(2,1)}, u32[]{:S(2)}) copy-start(bf16[1024,512]{1,0:T(8,128)(2,1)} %param.15) | copy-start | bytes 3145732
  259.9 86.0 %all-gather.14.cloned.1.call-start = ((), (), s32[]{:S(2)}) async-start(), calls=%async_computation.8 | async-start | bytes 5242880 | tf_op jit(solution)/shard_map/all_gather | solution.py:388
  311.2 129.6 %all-gather.16.cloned.1.call-start = ((), (), s32[]{:S(2)}) async-start(), calls=%async_computation.9 | async-start | bytes 6488064 | tf_op jit(solution)/shard_map/all_gather | solution.py:392
  311.8 223.1 %all-gather.20.cloned.1.call-start = ((), (), s32[]{:S(2)}) async-start(), calls=%async_computation.11 | async-start | bytes 6488064 | tf_op jit(solution)/shard_map/all_gather | solution.py:403
  312.6 315.6 %all-gather.18.cloned.1.call-start = ((), (), s32[]{:S(2)}) async-start(), calls=%async_computation.10 | async-start | bytes 6488064 | tf_op jit(solution)/shard_map/all_gather | solution.py:397
  313.3 394.7 %reduce-scatter.5.cloned.1.call-start = ((), (), s32[]{:S(2)}) async-start(), calls=%async_computation.12 | async-start | bytes 5242880 | tf_op jit(solution)/shard_map/reduce_scatter | solution.py:406
  649.0 59.0 %copy-start.5 = (bf16[1024,512]{1,0:T(8,128)(2,1)S(1)}, bf16[1024,512]{1,0:T(8,128)(2,1)}, u32[]{:S(2)}) copy-start(bf16[1024,512]{1,0:T(8,128)(2,1)} %add_convert_fusion.1) | copy-start | bytes 3145732
  649.1 61.5 %copy-start.1 = (bf16[2048,4]{0,1:T(4,128)(2,1)S(1)}, bf16[2048,4]{0,1:T(4,128)(2,1)}, u32[]{:S(2)}) copy-start(bf16[2048,4]{0,1:T(4,128)(2,1)} %param.20) | copy-start | bytes 49156
  649.1 51.5 %all-to-all-start.1 = ((bf16[16,4,128,128]{3,2,1,0:T(8,128)(2,1)}), bf16[16,4,128,128]{3,2,1,0:T(8,128)(2,1)S(1)}, u32[]{:S(2)}, u32[]{:S(2)}) async-start(bf16[16,4,128,128]{3,2,1,0:T(8,128)(2,1)} %get-tuple-element.14), calls=%async_computation.1 | async-start | bytes 4194304 | tf_op jit(solution)/shard_map/all_to_all | solution.py:378
  (2 other events, 5.6 us)
Sparse Core Ops, SparseCore 0:
  9.6 45.5 all-gather.7
  57.4 99.0 all-gather.9
  158.6 50.5 all-gather.11
  260.0 48.6 reduce-scatter.2
  311.4 34.4 all-gather.13
  348.1 92.6 all-gather.15
  443.1 91.7 all-gather.19
  537.3 90.8 all-gather.17
  649.2 42.6 reduce-scatter.4

commit v2 on v1

--- a/solution.py
+++ b/solution.py
@@ -18,6 +18,38 @@
     count = lax.axis_size(axis)
     initial, last = (max(0, -steps), min(count, count - steps))
     return lax.ppermute(value, axis, [(source, source + steps) for source in range(initial, last)])
+
+
+def swap(value, bit):
+    return lax.ppermute(value, "mp", [(i, i ^ bit) for i in range(lax.axis_size("mp"))])
+
+
+def share_columns(block):
+    me = lax.axis_index("mp")
+    held = [block]
+    bit = lax.axis_size("mp") // 2
+    while bit:
+        low = (me & bit) == 0
+        pairs = [(entry, swap(entry, bit)) for entry in held]
+        held = [part for e, g in pairs for part in (jnp.where(low, e, g), jnp.where(low, g, e))]
+        bit //= 2
+    return jnp.concatenate(held, axis=1)
+
+
+def product_shared(rows, weight):
+    me = lax.axis_index("mp")
+    count = lax.axis_size("mp")
+    part = weight.shape[1] // count
+    terms = {}
+    for apart in range(count):
+        piece = lax.dynamic_slice_in_dim(weight, (me ^ apart) * part, part, 1)
+        terms[apart] = jnp.dot(rows, piece, preferred_element_type=F32)
+    bit = 1
+    while bit < count // 2:
+        got = {r ^ bit: swap(terms[r].astype(BF16), bit) for r in sorted(terms, reverse=True) if r & bit}
+        terms = {r: terms[r] + got[r].astype(F32) for r in sorted(got)}
+        bit *= 2
+    return terms[0], swap(terms[bit].astype(BF16), bit)
 
 
 def normalize_rows(matrix, scaling):
@@ -334,7 +366,7 @@
     dk = prior_states.shape[2]
     requests = prior_states.shape[0]
     joined_width = 3 * dk
-    gathered = lax.all_gather(tokens, "mp", axis=1, tiled=True)
+    gathered = share_columns(tokens)
     token_total = gathered.shape[0]
     spans = token_total // SPAN
     heads_of = jnp.arange(head_total, dtype=jnp.int32)
@@ -369,6 +401,11 @@
     query, base, decay, add = intra(
         begins, behind, projected, conv_weight, gating_all, local_heads, dk
     )
+    o_full = lax.all_gather(o_weight, "group", axis=1, tiled=True)
+    gate_full = lax.all_gather(gate_weight, "group", axis=0, tiled=True)
+    up_full = lax.all_gather(up_weight, "group", axis=0, tiled=True)
+    down_full = lax.all_gather(down_weight, "group", axis=1, tiled=True)
+    decay, o_full = lax.optimization_barrier((decay, o_full))
     last = tail(starts[-1:].astype(jnp.int32), decay, add, prior_states)
     handed = from_behind(last, "group", 1)
     attended, leaving = scan(
@@ -376,35 +413,18 @@
         prior_states, handed, out_gain[None], group_count * CAP,
     )
     arrived = lax.all_to_all(leaving, "group", split_axis=0, concat_axis=0, tiled=True)
+    kept, got = product_shared(attended, o_full)
+    got, gate_full = lax.optimization_barrier((got, gate_full))
+    residual_one = (tokens.astype(F32) + (kept + got.astype(F32))).astype(BF16)
+    mixed_rows = share_columns(residual_one)
+    post_normed = normalize_rows(mixed_rows, 1.0).astype(BF16)
+    gate_part = jnp.dot(post_normed, gate_full, preferred_element_type=F32)
+    up_part = jnp.dot(post_normed, up_full, preferred_element_type=F32)
+    hidden = (jax.nn.silu(gate_part) * up_part).astype(BF16)
+    hidden, arrived = lax.optimization_barrier((hidden, arrived))
     state_pages = place(incoming, arrived, requests)
-
-    mixer_terms = jnp.dot(
-        attended,
-        lax.all_gather(o_weight, "group", axis=1, tiled=True),
-        preferred_element_type=F32,
-    ).astype(BF16)
-    mixer_sum = lax.psum_scatter(mixer_terms, "mp", scatter_dimension=1, tiled=True).astype(F32)
-    residual_one = (tokens.astype(F32) + mixer_sum).astype(BF16)
-    mixed_rows = lax.all_gather(residual_one, "mp", axis=1, tiled=True)
-    post_normed = normalize_rows(mixed_rows, 1.0).astype(BF16)
-    gate_part = jnp.dot(
-        post_normed,
-        lax.all_gather(gate_weight, "group", axis=0, tiled=True),
-        preferred_element_type=F32,
-    )
-    up_part = jnp.dot(
-        post_normed,
-        lax.all_gather(up_weight, "group", axis=0, tiled=True),
-        preferred_element_type=F32,
-    )
-    hidden = (jax.nn.silu(gate_part) * up_part).astype(BF16)
-    feed_terms = jnp.dot(
-        hidden,
-        lax.all_gather(down_weight, "group", axis=1, tiled=True),
-        preferred_element_type=F32,
-    ).astype(BF16)
-    feed_sum = lax.psum_scatter(feed_terms, "mp", scatter_dimension=1, tiled=True).astype(F32)
-    layer_out = (residual_one.astype(F32) + feed_sum).astype(BF16)
+    kept, got = product_shared(hidden, down_full)
+    layer_out = (residual_one.astype(F32) + (kept + got.astype(F32))).astype(BF16)
     return (attended, state_pages, layer_out)
 
 

time: 718 us -> 560 us (0.78)
  waiting for transfers between devices: 494 us -> 301 us
  local copies, waits for them, and re-layouts: 2.91 us -> 18 us
  starting transfers between devices: 11 us -> 24.4 us
  blocking collectives: 37.7 us -> 29 us
  matrix products: 51.1 us -> 58.5 us
    all_gather x6 -> x4, waiting for transfers between devices: 300 us -> 179 us  [the longest x1 81.6 us: shards(): down_full = lax.all_gather(down_weight, 'group', axis=1, tiled=True)]
    ppermute x0 -> x12, waiting for transfers between devices: none -> 63.4 us  [swap(): lax.ppermute(value, 'mp', [(i, i ^ bit) for i in range(lax.axis_size('mp'...]
    reduce_scatter x2 -> x0, waiting for transfers between devices: 48.8 us -> none  [the longest x1 48.8 us: shards(): lax.psum_scatter(mixer_terms, 'mp', scatter_dimension=1, tiled=True)]
    all_to_all x1, waiting for transfers between devices: 47.1 us -> 0.01 us  [shards(): lax.all_to_all(leaving, 'group', split_axis=0, concat_axis=0, tiled=True)]
    all_gather x1, waiting for transfers between devices: 92.7 us -> 51.5 us  [shards(): lax.all_gather(shared.reshape(-1, local_heads * joined_width), 'group', a...]
    unnamed x31 -> x85, local copies, waits for them, and re-layouts: 2.24 us -> 17.4 us
    select_n x0 -> x6, other arithmetic: none -> 10.8 us  [share_columns(): jnp.where(low, e, g)]
    all_to_all x1, blocking collectives: 25.5 us -> 16.5 us  [shards(): shared = lax.all_to_all(ordered, 'mp', split_axis=0, concat_axis=0)]
  transfers between devices with their start and end apart: 12 -> 20, of which waited for: 9 -> 10; matrix products, arithmetic and copies ran while one was open for 5% -> 13% of each run, Pallas kernels for 13% -> 15%
where the time goes in v2:
time: 560 us; the launch traced here: 558 us
  waiting for transfers between devices  301 us (54%)
  Pallas kernels  91.4 us (16%)
  matrix products  58.5 us (10%)
  blocking collectives  29 us (5%)
  starting transfers between devices  24.4 us (4%)
  other arithmetic  20.9 us (4%)
  local copies, waits for them, and re-layouts  18 us (3%)
  between operations  15.1 us (3%)
    all_gather x1, waiting for transfers between devices, shards(): down_full = lax.all_gather(down_weight, 'group', axis=1, tiled=True)  81.6 us
    all_gather x1, waiting for transfers between devices, shards(): up_full = lax.all_gather(up_weight, 'group', axis=0, tiled=True)  79.3 us
    pallas_call x1, Pallas kernels, intra(): pl.pallas_call(partial(intra_kernel, per, heads, dk), grid_spec=pltpu.Pre...  66 us
    ppermute x12, waiting for transfers between devices, swap(): lax.ppermute(value, 'mp', [(i, i ^ bit) for i in range(lax.axis_size('mp'...  63.4 us
    all_gather x1, waiting for transfers between devices, shards(): lax.all_gather(shared.reshape(-1, local_heads * joined_width), 'group', a...  51.5 us
    dot_general x8, matrix products, product_shared(): terms[apart] = jnp.dot(rows, piece, preferred_element_type=F32)  24.3 us
    all_gather x1, waiting for transfers between devices, shards(): gate_full = lax.all_gather(gate_weight, 'group', axis=0, tiled=True)  18 us
    unnamed x85, local copies, waits for them, and re-layouts  17.4 us
  transfers between devices with their start and end apart: 20, of which 10 were waited for; matrix products, arithmetic and copies ran while one was open for 13% of the time, Pallas kernels for 15%

profile of v2, /device:TPU:0, one launch (start us, length us, event | category | flops | bytes accessed | tf_op | source)
XLA Modules:
  0.0 558.3 jit_solution(5035508269402356230)
XLA Ops:
  8.6 10.0 %order_heads.1 = bf16[4,64,1536]{2,1,0:T(8,128)(2,1)} custom-call(s32[16]{0:T(128)} %select_reduce_fusion.2.slot_ref, f32[64,6144]{1,0:T(8,128)} %x_ref.1), custom_call_target="tpu_custom_call" | custom-call | tf_op jit(solution)/shard_map/order_heads/pallas_call | solution.py:90
  18.6 16.5 %all_to_all.10 = bf16[4,64,1536]{2,1,0:T(8,128)(2,1)} all-to-all(bf16[4,64,1536]{2,1,0:T(8,128)(2,1)} %order_heads.1), channel_id=1, replica_groups=mesh['group'=8,'mp'=4] {'mp'}, dimensions={0} | all-to-all | bytes 1572864 | tf_op jit(solution)/shard_map/all_to_all | solution.py:377
  37.7 24.2 %collective-permute-done = bf16[1024,512]{0,1:T(8,128)(2,1)} collective-permute-done((bf16[1024,512]{0,1:T(8,128)(2,1)S(1)}, bf16[1024,512]{0,1:T(8,128)(2,1)}, u32[]{:S(2)}, u32[]{:S(2)}) %collective-permute-start) | collective-permute-done | bytes 1048608 | tf_op jit(solution)/shard_map/ppermute | solution.py:24
  64.9 12.4 %all-reduce = s32[64]{0:T(128)S(1)} all-reduce(s32[64]{0:T(128)S(1)} %dynamic-update-slice), channel_id=1, replica_groups=mesh['group'=8,'mp'=4] {'group'}, use_global_device_ids=true, to_apply=%add | all-reduce | flops 64 | bytes 512
  84.0 51.5 %all-gather.6.cloned.1.call-done = bf16[2048,1536]{1,0:T(8,128)(2,1)} async-done(((bf16[256,1536]{1,0:T(8,128)(2,1)}), bf16[2048,1536]{1,0:T(8,128)(2,1)}) %all-gather.6.cloned.1.call-update) | async-done | bytes 6291472 | tf_op jit(solution)/shard_map/all_gather | solution.py:378
  135.5 10.7 %convolution_convert_fusion.before_ref.rows_ref = bf16[1024,1536]{1,0:T(8,128)(2,1)S(1)} fusion(bf16[2048,1536]{1,0:T(8,128)(2,1)} %all-gather.6.cloned.1.call-done, f32[2048]{0:T(1024)S(1)} %copy-done.32, f32[1024]{0:T(1024)S(1)} %add_rsqrt_fusion.1, bf16[1024,512]{0,1:T(8,128)(2,1)} %copy-done.18, bf16[1024,512]{0,1:T(8,128)(2,1)} %copy-done.16, ...), kind=kOutput, calls=%fused_computation.12 | convolution fusion | flops 6467092480 | bytes 13643776 | tf_op jit(solution)/shard_map/dot_general | solution.py:385
  150.9 66.0 %intra.1 = (bf16[16,256,128]{2,1,0:T(8,128)(2,1)S(1)}, f32[16,256,128]{2,1,0:T(8,128)S(1)}, bf16[16,4,128,128]{3,2,1,0:T(8,128)(2,1)S(1)}, f32[16,4,128,128]{3,2,1,0:T(8,128)S(1)}) custom-call(s32[16]{0:T(128)S(1)} %fusion.42.flags, bf16[16,1536]{1,0:T(8,128)(2,1)S(1)} %collective-permute-done.3.first_ref, ...), custom_call_target="tpu_custom_call" | custom-call | flops 60000002048 | bytes 200000000 | tf_op jit(solution)/shard_map/intra/pallas_call | solution.py:180
  226.1 3.9 collective-permute-start.4
  230.1 5.6 %collective-permute-done.4.handed_ref = bf16[4,128,128]{2,1,0:T(8,128)(2,1)S(1)} collective-permute-done((bf16[4,128,128]{2,1,0:T(8,128)(2,1)S(1)}, bf16[4,128,128]{2,1,0:T(8,128)(2,1)S(1)}, u32[]{:S(2)}, u32[]{:S(2)}) %collective-permute-start.4) | collective-permute-done | bytes 131104 | tf_op jit(solution)/shard_map/ppermute | solution.py:20
  241.2 8.5 %scan.1 = (bf16[1024,512]{1,0:T(8,128)(2,1)}, bf16[16,4,128,128]{3,2,1,0:T(8,128)(2,1)}) custom-call(s32[16]{0:T(128)S(1)} %broadcast_add_fusion.1.seg, s32[16]{0:T(128)S(1)} %convert_element_type.77.starts, s32[16]{0:T(128)S(1)} %select_reduce_fusion.3.dest, s32[1]{0:T(128)} %bitcast.2.linked, bf16[16,4,128,128]{3,2,1,0:T(8,128)(2,1)S(1)} %copy-done.8, ...), custom_call_target="tpu_custom_call" | custom-call | flops 10000000000 | bytes 40000000 | tf_op jit(solution)/shard_map/scan/pallas_call | solution.py:275
  254.6 3.1 add_convert_fusion.3
  259.1 2.8 convolution_convert_fusion.4
  262.0 3.2 fusion.28
  265.1 18.0 %all-gather.10.cloned.1.call-done = bf16[2048,1408]{1,0:T(8,128)(2,1)} async-done(((bf16[256,1408]{1,0:T(8,128)(2,1)}), bf16[2048,1408]{1,0:T(8,128)(2,1)}) %all-gather.10.cloned.1.call-update) | async-done | bytes 5767184 | tf_op jit(solution)/shard_map/all_gather | solution.py:405
  287.3 22.9 %collective-permute-done.8 = bf16[1024,512]{0,1:T(8,128)(2,1)S(1)} collective-permute-done((bf16[1024,512]{0,1:T(8,128)(2,1)S(1)}, bf16[1024,512]{0,1:T(8,128)(2,1)S(1)}, u32[]{:S(2)}, u32[]{:S(2)}) %collective-permute-start.8) | collective-permute-done | bytes 1048608 | tf_op jit(solution)/shard_map/ppermute | solution.py:24
  312.2 12.3 %all-to-all-start.1 = ((bf16[16,4,128,128]{3,2,1,0:T(8,128)(2,1)}), bf16[16,4,128,128]{3,2,1,0:T(8,128)(2,1)S(1)}, u32[]{:S(2)}, u32[]{:S(2)}) async-start(bf16[16,4,128,128]{3,2,1,0:T(8,128)(2,1)} %get-tuple-element.24), calls=%async_computation.1 | async-start | bytes 4194304 | tf_op jit(solution)/shard_map/all_to_all | solution.py:415
  330.3 8.7 %fusion.7 = f32[1024,1408]{1,0:T(8,128)} fusion(bf16[2048,1408]{1,0:T(8,128)(2,1)S(1)} %bitcast.20, f32[1024]{0:T(1024)S(1)} %add_rsqrt_fusion, bf16[1024,512]{0,1:T(8,128)(2,1)S(1)} %get-tuple-element.41, bf16[1024,512]{0,1:T(8,128)(2,1)S(1)} %get-tuple-element.40, bf16[1024,512]{0,1:T(8,128)(2,1)S(1)} %get-tuple-element.37, ...), kind=kOutput, calls=%fused_computation.14 | convolution fusion | flops 5926551552 | bytes 15732736 | tf_op jit(solution)/shard_map/dot_general | solution.py:421
  339.0 79.3 %all-gather.12.cloned.1.call-done = bf16[2048,1408]{1,0:T(8,128)(2,1)} async-done(((bf16[256,1408]{1,0:T(8,128)(2,1)}), bf16[2048,1408]{1,0:T(8,128)(2,1)}) %all-gather.12.cloned.1.call-update) | async-done | bytes 5767184 | tf_op jit(solution)/shard_map/all_gather | solution.py:406
  418.3 13.0 %multiply_convert_fusion = bf16[1024,1408]{1,0:T(8,128)(2,1)} fusion(f32[1024,1408]{1,0:T(8,128)} %fusion.7, bf16[2048,1408]{1,0:T(8,128)(2,1)} %all-gather.12.cloned.1.call-done, f32[1024]{0:T(1024)S(1)} %add_rsqrt_fusion, bf16[1024,512]{0,1:T(8,128)(2,1)} %copy-done.21, bf16[1024,512]{0,1:T(8,128)(2,1)} %copy-done.20, bf16[1024,512]{0,1:T(8,128)(2,1)} %copy-done.25, ...), kind=kOutput, calls=%fused_computation.9 | convolution fusion | flops 5935202304 | bytes 18616320 | tf_op jit(solution)/shard_map/dot_general | solution.py:422
  431.4 81.6 %all-gather.14.cloned.1.call-done = bf16[1408,2048]{1,0:T(8,128)(2,1)} async-done(((bf16[1408,256]{1,0:T(8,128)(2,1)}), bf16[1408,2048]{1,0:T(8,128)(2,1)}) %all-gather.14.cloned.1.call-update) | async-done | bytes 5767184 | tf_op jit(solution)/shard_map/all_gather | solution.py:407
  512.9 4.2 convolution_convert_fusion.1
  524.8 6.1 %place.1 = f32[8,4,128,128]{3,2,1,0:T(8,128)} custom-call(s32[8]{0:T(128)} %select_reduce_fusion.index, bf16[16,4,128,128]{3,2,1,0:T(8,128)(2,1)} %copy-done.15), custom_call_target="tpu_custom_call" | custom-call | tf_op jit(solution)/shard_map/place/pallas_call | solution.py:313
  530.9 4.1 fusion.15
  535.0 13.5 %collective-permute-done.13 = bf16[1024,512]{0,1:T(8,128)(2,1)} collective-permute-done((bf16[1024,512]{0,1:T(8,128)(2,1)}, bf16[1024,512]{0,1:T(8,128)(2,1)}, u32[]{:S(2)}, u32[]{:S(2)}) %collective-permute-start.13) | collective-permute-done | bytes 1048608 | tf_op jit(solution)/shard_map/ppermute | solution.py:24
  (158 shorter events, 61.0 us)
Async XLA Ops:
  7.2 141.8 %copy-start = (bf16[2048,4]{0,1:T(4,128)(2,1)S(1)}, bf16[2048,4]{0,1:T(4,128)(2,1)}, u32[]{:S(2)}) copy-start(bf16[2048,4]{0,1:T(4,128)(2,1)} %param.20) | copy-start | bytes 49156
  7.2 128.3 %all-gather.6.cloned.1.call-start = ((), (), s32[]{:S(2)}) async-start(), calls=%async_computation.2 | async-start | bytes 7077888 | tf_op jit(solution)/shard_map/all_gather | solution.py:378
  35.2 186.4 %all-gather.8.cloned.1.call-start = ((), (), s32[]{:S(2)}) async-start(), calls=%async_computation.3 | async-start | bytes 2359296 | tf_op jit(solution)/shard_map/all_gather | solution.py:404
  35.9 247.2 %all-gather.10.cloned.1.call-start = ((), (), s32[]{:S(2)}) async-start(), calls=%async_computation.4 | async-start | bytes 6488064 | tf_op jit(solution)/shard_map/all_gather | solution.py:405
  36.7 381.7 %all-gather.12.cloned.1.call-start = ((), (), s32[]{:S(2)}) async-start(), calls=%async_computation.5 | async-start | bytes 6488064 | tf_op jit(solution)/shard_map/all_gather | solution.py:406
  37.3 24.7 %collective-permute-start = (bf16[1024,512]{0,1:T(8,128)(2,1)S(1)}, bf16[1024,512]{0,1:T(8,128)(2,1)}, u32[]{:S(2)}, u32[]{:S(2)}) collective-permute-start(bf16[1024,512]{0,1:T(8,128)(2,1)S(1)} %copy.45), channel_id=1, source_target_pairs={{0,2},{1,3},{2,0},{3,1},{4,6},{5,7},{6,4},{7,5},{8,10},{9,11},{10,... | collective-permute-start | bytes 3145736 | tf_op jit(solution)/shard_map/ppermute | solution.py:24
  37.4 475.6 %all-gather.14.cloned.1.call-start = ((), (), s32[]{:S(2)}) async-start(), calls=%async_computation.6 | async-start | bytes 6488064 | tf_op jit(solution)/shard_map/all_gather | solution.py:407
  63.3 15.9 %collective-permute-start.2 = (bf16[1024,512]{0,1:T(8,128)(2,1)S(1)}, bf16[1024,512]{0,1:T(8,128)(2,1)}, u32[]{:S(2)}, u32[]{:S(2)}) collective-permute-start(bf16[1024,512]{0,1:T(8,128)(2,1)S(1)} %get-tuple-element.45), channel_id=1, source_target_pairs={{0,1},{1,0},{2,3},{3,2},{4,5},{5,4},{6,7},{7,6},{8,9},{9,8},{10,11... | collective-permute-start | bytes 3145736 | tf_op jit(solution)/shard_map/ppermute | solution.py:24
  77.5 3.2 collective-permute-start.1
  84.0 65.0 %copy-start.17 = (bf16[1024,512]{0,1:T(8,128)(2,1)S(1)}, bf16[1024,512]{0,1:T(8,128)(2,1)}, u32[]{:S(2)}) copy-start(bf16[1024,512]{0,1:T(8,128)(2,1)} %copy-done.16) | copy-start | bytes 3145732
  146.3 4.6 collective-permute-start.3
  150.8 70.7 %copy-start.5 = (f32[8,4,128,128]{3,2,1,0:T(8,128)S(1)}, f32[8,4,128,128]{3,2,1,0:T(8,128)}, u32[]{:S(2)}) copy-start(f32[8,4,128,128]{3,2,1,0:T(8,128)} %prior_ref.3) | copy-start | bytes 6291460
  226.1 9.6 %collective-permute-start.4 = (bf16[4,128,128]{2,1,0:T(8,128)(2,1)S(1)}, bf16[4,128,128]{2,1,0:T(8,128)(2,1)S(1)}, u32[]{:S(2)}, u32[]{:S(2)}) collective-permute-start(bf16[4,128,128]{2,1,0:T(8,128)(2,1)S(1)} %tail.1), channel_id=1, source_target_pairs={{0,4},{4,8},{8,12},{12,16},{16,20},{20,24},{24,28},{1,5},{5,9},{9,... | collective-permute-start | bytes 393224 | tf_op jit(solution)/shard_map/ppermute | solution.py:20
  251.8 2.7 collective-permute-start.6
  257.7 25.5 %collective-permute-start.7 = (bf16[1024,512]{0,1:T(8,128)(2,1)}, bf16[1024,512]{0,1:T(8,128)(2,1)S(1)}, u32[]{:S(2)}, u32[]{:S(2)}) collective-permute-start(bf16[1024,512]{0,1:T(8,128)(2,1)} %add_convert_fusion.3), channel_id=1, source_target_pairs={{0,2},{1,3},{2,0},{3,1},{4,6},{5,7},{6,4},{7,5},{8,10},{9,11},{10,... | collective-permute-start | bytes 3145736 | tf_op jit(solution)/shard_map/ppermute | solution.py:24
  262.0 21.2 %collective-permute-start.5 = (bf16[1024,512]{0,1:T(8,128)(2,1)}, bf16[1024,512]{0,1:T(8,128)(2,1)}, u32[]{:S(2)}, u32[]{:S(2)}) collective-permute-start(bf16[1024,512]{0,1:T(8,128)(2,1)} %convolution_convert_fusion.4), channel_id=1, source_target_pairs={{0,1},{1,0},{2,3},{3,2},{4,5},{5,4},{6,7},{7,6},{8,9},{9,8},{10,11... | collective-permute-start | bytes 3145736 | tf_op jit(solution)/shard_map/ppermute | solution.py:24
  285.8 24.4 %collective-permute-start.8 = (bf16[1024,512]{0,1:T(8,128)(2,1)S(1)}, bf16[1024,512]{0,1:T(8,128)(2,1)S(1)}, u32[]{:S(2)}, u32[]{:S(2)}) collective-permute-start(bf16[1024,512]{0,1:T(8,128)(2,1)S(1)} %add_convert_fusion.2), channel_id=1, source_target_pairs={{0,2},{1,3},{2,0},{3,1},{4,6},{5,7},{6,4},{7,5},{8,10},{9,11},{10,... | collective-permute-start | bytes 3145736 | tf_op jit(solution)/shard_map/ppermute | solution.py:24
  311.7 12.8 %collective-permute-start.10 = (bf16[1024,512]{0,1:T(8,128)(2,1)}, bf16[1024,512]{0,1:T(8,128)(2,1)}, u32[]{:S(2)}, u32[]{:S(2)}) collective-permute-start(bf16[1024,512]{0,1:T(8,128)(2,1)} %get-tuple-element.39), channel_id=1, source_target_pairs={{0,1},{1,0},{2,3},{3,2},{4,5},{5,4},{6,7},{7,6},{8,9},{9,8},{10,11... | collective-permute-start | bytes 3145736 | tf_op jit(solution)/shard_map/ppermute | solution.py:24
  311.7 14.7 %collective-permute-start.9 = (bf16[1024,512]{0,1:T(8,128)(2,1)}, bf16[1024,512]{0,1:T(8,128)(2,1)}, u32[]{:S(2)}, u32[]{:S(2)}) collective-permute-start(bf16[1024,512]{0,1:T(8,128)(2,1)} %get-tuple-element.38), channel_id=1, source_target_pairs={{0,1},{1,0},{2,3},{3,2},{4,5},{5,4},{6,7},{7,6},{8,9},{9,8},{10,11... | collective-permute-start | bytes 3145736 | tf_op jit(solution)/shard_map/ppermute | solution.py:24
  312.2 119.2 %all-to-all-start.1 = ((bf16[16,4,128,128]{3,2,1,0:T(8,128)(2,1)}), bf16[16,4,128,128]{3,2,1,0:T(8,128)(2,1)S(1)}, u32[]{:S(2)}, u32[]{:S(2)}) async-start(bf16[16,4,128,128]{3,2,1,0:T(8,128)(2,1)} %get-tuple-element.24), calls=%async_computation.1 | async-start | bytes 4194304 | tf_op jit(solution)/shard_map/all_to_all | solution.py:415
  431.4 85.8 %copy-start.15 = (bf16[16,4,128,128]{3,2,1,0:T(8,128)(2,1)}, bf16[16,4,128,128]{3,2,1,0:T(8,128)(2,1)S(1)}, u32[]{:S(2)}) copy-start(bf16[16,4,128,128]{3,2,1,0:T(8,128)(2,1)S(1)} %all-to-all-done.1.x_ref) | copy-start | bytes 6291460
  517.1 2.7 collective-permute-start.12
  519.6 15.3 %collective-permute-start.11 = (bf16[1024,512]{0,1:T(8,128)(2,1)S(1)}, bf16[1024,512]{0,1:T(8,128)(2,1)S(1)}, u32[]{:S(2)}, u32[]{:S(2)}) collective-permute-start(bf16[1024,512]{0,1:T(8,128)(2,1)S(1)} %convolution_convert_fusion.2), channel_id=1, source_target_pairs={{0,1},{1,0},{2,3},{3,2},{4,5},{5,4},{6,7},{7,6},{8,9},{9,8},{10,11... | collective-permute-start | bytes 3145736 | tf_op jit(solution)/shard_map/ppermute | solution.py:24
  522.7 25.7 %collective-permute-start.13 = (bf16[1024,512]{0,1:T(8,128)(2,1)}, bf16[1024,512]{0,1:T(8,128)(2,1)}, u32[]{:S(2)}, u32[]{:S(2)}) collective-permute-start(bf16[1024,512]{0,1:T(8,128)(2,1)} %add_convert_fusion.1), channel_id=1, source_target_pairs={{0,2},{1,3},{2,0},{3,1},{4,6},{5,7},{6,4},{7,5},{8,10},{9,11},{10,... | collective-permute-start | bytes 3145736 | tf_op jit(solution)/shard_map/ppermute | solution.py:24
  (36 other events, 493.1 us)
Sparse Core Ops, SparseCore 0:
  35.3 100.2 all-gather.5
  137.6 50.5 all-gather.7
  190.3 92.7 all-gather.9
  285.2 133.1 all-gather.11
  420.2 92.6 all-gather.13

commit v3 on v2

--- a/solution.py
+++ b/solution.py
@@ -401,7 +401,7 @@
     query, base, decay, add = intra(
         begins, behind, projected, conv_weight, gating_all, local_heads, dk
     )
-    o_full = lax.all_gather(o_weight, "group", axis=1, tiled=True)
+    o_full = lax.all_gather(o_weight, "group", axis=0)
     gate_full = lax.all_gather(gate_weight, "group", axis=0, tiled=True)
     up_full = lax.all_gather(up_weight, "group", axis=0, tiled=True)
     down_full = lax.all_gather(down_weight, "group", axis=1, tiled=True)
@@ -413,6 +413,7 @@
         prior_states, handed, out_gain[None], group_count * CAP,
     )
     arrived = lax.all_to_all(leaving, "group", split_axis=0, concat_axis=0, tiled=True)
+    o_full = o_full.transpose(1, 0, 2).reshape(o_weight.shape[0], -1)
     kept, got = product_shared(attended, o_full)
     got, gate_full = lax.optimization_barrier((got, gate_full))
     residual_one = (tokens.astype(F32) + (kept + got.astype(F32))).astype(BF16)

time: 560 us -> 558 us (level)
  waiting for transfers between devices: 301 us -> 294 us
  transfers between devices with their start and end apart: 20 -> 20, of which waited for: 10 -> 11; matrix products, arithmetic and copies ran while one was open for 13% -> 14% of each run, Pallas kernels for 15% -> 15%
where the time goes in v3:
time: 558 us; the launch traced here: 556 us
  waiting for transfers between devices  294 us (53%)
  Pallas kernels  91.4 us (16%)
  matrix products  58.4 us (10%)
  blocking collectives  29 us (5%)
  starting transfers between devices  25.2 us (5%)
  local copies, waits for them, and re-layouts  22 us (4%)
  other arithmetic  20.9 us (4%)
  between operations  15.1 us (3%)
    all_gather x1, waiting for transfers between devices, shards(): down_full = lax.all_gather(down_weight, 'group', axis=1, tiled=True)  81.6 us
    all_gather x1, waiting for transfers between devices, shards(): up_full = lax.all_gather(up_weight, 'group', axis=0, tiled=True)  76.5 us
    pallas_call x1, Pallas kernels, intra(): pl.pallas_call(partial(intra_kernel, per, heads, dk), grid_spec=pltpu.Pre...  66 us
    ppermute x12, waiting for transfers between devices, swap(): lax.ppermute(value, 'mp', [(i, i ^ bit) for i in range(lax.axis_size('mp'...  64.8 us
    all_gather x1, waiting for transfers between devices, shards(): lax.all_gather(shared.reshape(-1, local_heads * joined_width), 'group', a...  51.5 us
    dot_general x8, matrix products, product_shared(): terms[apart] = jnp.dot(rows, piece, preferred_element_type=F32)  24.1 us
    unnamed x85, local copies, waits for them, and re-layouts  17.4 us
    all_gather x1, waiting for transfers between devices, shards(): gate_full = lax.all_gather(gate_weight, 'group', axis=0, tiled=True)  16.6 us
  transfers between devices with their start and end apart: 20, of which 11 were waited for; matrix products, arithmetic and copies ran while one was open for 14% of the time, Pallas kernels for 15%

profile of v3, /device:TPU:0, one launch (start us, length us, event | category | flops | bytes accessed | tf_op | source)
XLA Modules:
  0.0 556.1 jit_solution(7086804357937193931)
XLA Ops:
  8.6 10.0 %order_heads.1 = bf16[4,64,1536]{2,1,0:T(8,128)(2,1)} custom-call(s32[16]{0:T(128)} %select_reduce_fusion.2.slot_ref, f32[64,6144]{1,0:T(8,128)} %x_ref.1), custom_call_target="tpu_custom_call" | custom-call | tf_op jit(solution)/shard_map/order_heads/pallas_call | solution.py:90
  18.6 16.5 %all_to_all.10 = bf16[4,64,1536]{2,1,0:T(8,128)(2,1)} all-to-all(bf16[4,64,1536]{2,1,0:T(8,128)(2,1)} %order_heads.1), channel_id=1, replica_groups=mesh['group'=8,'mp'=4] {'mp'}, dimensions={0} | all-to-all | bytes 1572864 | tf_op jit(solution)/shard_map/all_to_all | solution.py:377
  37.7 24.2 %collective-permute-done = bf16[1024,512]{0,1:T(8,128)(2,1)} collective-permute-done((bf16[1024,512]{0,1:T(8,128)(2,1)S(1)}, bf16[1024,512]{0,1:T(8,128)(2,1)}, u32[]{:S(2)}, u32[]{:S(2)}) %collective-permute-start) | collective-permute-done | bytes 1048608 | tf_op jit(solution)/shard_map/ppermute | solution.py:24
  64.9 12.4 %all-reduce = s32[64]{0:T(128)S(1)} all-reduce(s32[64]{0:T(128)S(1)} %dynamic-update-slice), channel_id=1, replica_groups=mesh['group'=8,'mp'=4] {'group'}, use_global_device_ids=true, to_apply=%add | all-reduce | flops 64 | bytes 512
  84.0 51.5 %all-gather.7.cloned.1.call-done = bf16[2048,1536]{1,0:T(8,128)(2,1)} async-done(((bf16[256,1536]{1,0:T(8,128)(2,1)}), bf16[2048,1536]{1,0:T(8,128)(2,1)}) %all-gather.7.cloned.1.call-update) | async-done | bytes 6291472 | tf_op jit(solution)/shard_map/all_gather | solution.py:378
  135.5 10.7 %convolution_convert_fusion.before_ref.rows_ref = bf16[1024,1536]{1,0:T(8,128)(2,1)S(1)} fusion(bf16[2048,1536]{1,0:T(8,128)(2,1)} %all-gather.7.cloned.1.call-done, f32[2048]{0:T(1024)S(1)} %copy-done.32, f32[1024]{0:T(1024)S(1)} %add_rsqrt_fusion.1, bf16[1024,512]{0,1:T(8,128)(2,1)} %copy-done.18, bf16[1024,512]{0,1:T(8,128)(2,1)} %copy-done.16, ...), kind=kOutput, calls=%fused_computation.12 | convolution fusion | flops 6467092480 | bytes 13643776 | tf_op jit(solution)/shard_map/dot_general | solution.py:385
  150.9 66.0 %intra.1 = (bf16[16,256,128]{2,1,0:T(8,128)(2,1)S(1)}, f32[16,256,128]{2,1,0:T(8,128)S(1)}, bf16[16,4,128,128]{3,2,1,0:T(8,128)(2,1)S(1)}, f32[16,4,128,128]{3,2,1,0:T(8,128)S(1)}) custom-call(s32[16]{0:T(128)S(1)} %fusion.42.flags, bf16[16,1536]{1,0:T(8,128)(2,1)S(1)} %collective-permute-done.3.first_ref, ...), custom_call_target="tpu_custom_call" | custom-call | flops 60000002048 | bytes 200000000 | tf_op jit(solution)/shard_map/intra/pallas_call | solution.py:180
  226.1 4.0 collective-permute-start.4
  230.2 4.0 copy.79
  241.3 8.5 %scan.1 = (bf16[1024,512]{1,0:T(8,128)(2,1)}, bf16[16,4,128,128]{3,2,1,0:T(8,128)(2,1)}) custom-call(s32[16]{0:T(128)S(1)} %broadcast_add_fusion.1.seg, s32[16]{0:T(128)S(1)} %convert_element_type.77.starts, s32[16]{0:T(128)S(1)} %select_reduce_fusion.3.dest, s32[1]{0:T(128)} %bitcast.2.linked, bf16[16,4,128,128]{3,2,1,0:T(8,128)(2,1)S(1)} %copy-done.8, ...), custom_call_target="tpu_custom_call" | custom-call | flops 10000000000 | bytes 40000000 | tf_op jit(solution)/shard_map/scan/pallas_call | solution.py:275
  254.7 3.1 add_convert_fusion.3
  259.3 2.8 convolution_convert_fusion.4
  262.1 3.1 fusion.28
  265.2 16.6 %all-gather.9.cloned.1.call-done = bf16[2048,1408]{1,0:T(8,128)(2,1)} async-done(((bf16[256,1408]{1,0:T(8,128)(2,1)}), bf16[2048,1408]{1,0:T(8,128)(2,1)}) %all-gather.9.cloned.1.call-update) | async-done | bytes 5767184 | tf_op jit(solution)/shard_map/all_gather | solution.py:405
  287.4 22.9 %collective-permute-done.8 = bf16[1024,512]{0,1:T(8,128)(2,1)S(1)} collective-permute-done((bf16[1024,512]{0,1:T(8,128)(2,1)S(1)}, bf16[1024,512]{0,1:T(8,128)(2,1)S(1)}, u32[]{:S(2)}, u32[]{:S(2)}) %collective-permute-start.8) | collective-permute-done | bytes 1048608 | tf_op jit(solution)/shard_map/ppermute | solution.py:24
  312.2 12.9 %all-to-all-start.1 = ((bf16[16,4,128,128]{3,2,1,0:T(8,128)(2,1)}), bf16[16,4,128,128]{3,2,1,0:T(8,128)(2,1)S(1)}, u32[]{:S(2)}, u32[]{:S(2)}) async-start(bf16[16,4,128,128]{3,2,1,0:T(8,128)(2,1)} %get-tuple-element.24), calls=%async_computation.1 | async-start | bytes 4194304 | tf_op jit(solution)/shard_map/all_to_all | solution.py:415
  330.8 8.7 %fusion.7 = f32[1024,1408]{1,0:T(8,128)} fusion(bf16[2048,1408]{1,0:T(8,128)(2,1)S(1)} %bitcast.28, f32[1024]{0:T(1024)S(1)} %add_rsqrt_fusion, bf16[1024,512]{0,1:T(8,128)(2,1)S(1)} %get-tuple-element.47, bf16[1024,512]{0,1:T(8,128)(2,1)S(1)} %get-tuple-element.46, bf16[1024,512]{0,1:T(8,128)(2,1)S(1)} %get-tuple-element.43, ...), kind=kOutput, calls=%fused_computation.14 | convolution fusion | flops 5926551552 | bytes 15732736 | tf_op jit(solution)/shard_map/dot_general | solution.py:422
  339.6 76.5 %all-gather.11.cloned.1.call-done = bf16[2048,1408]{1,0:T(8,128)(2,1)} async-done(((bf16[256,1408]{1,0:T(8,128)(2,1)}), bf16[2048,1408]{1,0:T(8,128)(2,1)}) %all-gather.11.cloned.1.call-update) | async-done | bytes 5767184 | tf_op jit(solution)/shard_map/all_gather | solution.py:406
  416.1 13.0 %multiply_convert_fusion = bf16[1024,1408]{1,0:T(8,128)(2,1)} fusion(f32[1024,1408]{1,0:T(8,128)} %fusion.7, bf16[2048,1408]{1,0:T(8,128)(2,1)} %all-gather.11.cloned.1.call-done, f32[1024]{0:T(1024)S(1)} %add_rsqrt_fusion, bf16[1024,512]{0,1:T(8,128)(2,1)} %copy-done.21, bf16[1024,512]{0,1:T(8,128)(2,1)} %copy-done.20, bf16[1024,512]{0,1:T(8,128)(2,1)} %copy-done.25, ...), kind=kOutput, calls=%fused_computation.9 | convolution fusion | flops 5935202304 | bytes 18616320 | tf_op jit(solution)/shard_map/dot_general | solution.py:423
  429.1 81.6 %all-gather.13.cloned.1.call-done = bf16[1408,2048]{1,0:T(8,128)(2,1)} async-done(((bf16[1408,256]{1,0:T(8,128)(2,1)}), bf16[1408,2048]{1,0:T(8,128)(2,1)}) %all-gather.13.cloned.1.call-update) | async-done | bytes 5767184 | tf_op jit(solution)/shard_map/all_gather | solution.py:407
  510.7 4.2 convolution_convert_fusion.1
  522.6 6.1 %place.1 = f32[8,4,128,128]{3,2,1,0:T(8,128)} custom-call(s32[8]{0:T(128)} %select_reduce_fusion.index, bf16[16,4,128,128]{3,2,1,0:T(8,128)(2,1)} %copy-done.15), custom_call_target="tpu_custom_call" | custom-call | tf_op jit(solution)/shard_map/place/pallas_call | solution.py:313
  528.7 4.1 fusion.15
  532.8 13.5 %collective-permute-done.13 = bf16[1024,512]{0,1:T(8,128)(2,1)} collective-permute-done((bf16[1024,512]{0,1:T(8,128)(2,1)}, bf16[1024,512]{0,1:T(8,128)(2,1)}, u32[]{:S(2)}, u32[]{:S(2)}) %collective-permute-start.13) | collective-permute-done | bytes 1048608 | tf_op jit(solution)/shard_map/ppermute | solution.py:24
  (159 shorter events, 64.0 us)
Async XLA Ops:
  7.2 141.8 %copy-start = (bf16[2048,4]{0,1:T(4,128)(2,1)S(1)}, bf16[2048,4]{0,1:T(4,128)(2,1)}, u32[]{:S(2)}) copy-start(bf16[2048,4]{0,1:T(4,128)(2,1)} %param.20) | copy-start | bytes 49156
  7.2 128.3 %all-gather.7.cloned.1.call-start = ((), (), s32[]{:S(2)}) async-start(), calls=%async_computation.2 | async-start | bytes 7077888 | tf_op jit(solution)/shard_map/all_gather | solution.py:378
  35.2 186.4 %all-gather.15.cloned.1.call-start = ((), (), s32[]{:S(2)}) async-start(), calls=%async_computation.6 | async-start | bytes 2359296 | tf_op jit(solution)/shard_map/all_gather | solution.py:404
  35.9 245.9 %all-gather.9.cloned.1.call-start = ((), (), s32[]{:S(2)}) async-start(), calls=%async_computation.3 | async-start | bytes 6488064 | tf_op jit(solution)/shard_map/all_gather | solution.py:405
  36.7 379.4 %all-gather.11.cloned.1.call-start = ((), (), s32[]{:S(2)}) async-start(), calls=%async_computation.4 | async-start | bytes 6488064 | tf_op jit(solution)/shard_map/all_gather | solution.py:406
  37.3 24.7 %collective-permute-start = (bf16[1024,512]{0,1:T(8,128)(2,1)S(1)}, bf16[1024,512]{0,1:T(8,128)(2,1)}, u32[]{:S(2)}, u32[]{:S(2)}) collective-permute-start(bf16[1024,512]{0,1:T(8,128)(2,1)S(1)} %copy.73), channel_id=1, source_target_pairs={{0,2},{1,3},{2,0},{3,1},{4,6},{5,7},{6,4},{7,5},{8,10},{9,11},{10,... | collective-permute-start | bytes 3145736 | tf_op jit(solution)/shard_map/ppermute | solution.py:24
  37.4 473.4 %all-gather.13.cloned.1.call-start = ((), (), s32[]{:S(2)}) async-start(), calls=%async_computation.5 | async-start | bytes 6488064 | tf_op jit(solution)/shard_map/all_gather | solution.py:407
  63.3 15.9 %collective-permute-start.2 = (bf16[1024,512]{0,1:T(8,128)(2,1)S(1)}, bf16[1024,512]{0,1:T(8,128)(2,1)}, u32[]{:S(2)}, u32[]{:S(2)}) collective-permute-start(bf16[1024,512]{0,1:T(8,128)(2,1)S(1)} %get-tuple-element.51), channel_id=1, source_target_pairs={{0,1},{1,0},{2,3},{3,2},{4,5},{5,4},{6,7},{7,6},{8,9},{9,8},{10,11... | collective-permute-start | bytes 3145736 | tf_op jit(solution)/shard_map/ppermute | solution.py:24
  77.5 3.2 collective-permute-start.1
  84.0 65.0 %copy-start.17 = (bf16[1024,512]{0,1:T(8,128)(2,1)S(1)}, bf16[1024,512]{0,1:T(8,128)(2,1)}, u32[]{:S(2)}) copy-start(bf16[1024,512]{0,1:T(8,128)(2,1)} %copy-done.16) | copy-start | bytes 3145732
  146.3 4.6 collective-permute-start.3
  150.8 70.7 %copy-start.5 = (f32[8,4,128,128]{3,2,1,0:T(8,128)S(1)}, f32[8,4,128,128]{3,2,1,0:T(8,128)}, u32[]{:S(2)}) copy-start(f32[8,4,128,128]{3,2,1,0:T(8,128)} %prior_ref.3) | copy-start | bytes 6291460
  226.1 9.8 %collective-permute-start.4 = (bf16[4,128,128]{2,1,0:T(8,128)(2,1)S(1)}, bf16[4,128,128]{2,1,0:T(8,128)(2,1)S(1)}, u32[]{:S(2)}, u32[]{:S(2)}) collective-permute-start(bf16[4,128,128]{2,1,0:T(8,128)(2,1)S(1)} %tail.1), channel_id=1, source_target_pairs={{0,4},{4,8},{8,12},{12,16},{16,20},{20,24},{24,28},{1,5},{5,9},{9,... | collective-permute-start | bytes 393224 | tf_op jit(solution)/shard_map/ppermute | solution.py:20
  252.0 2.7 collective-permute-start.6
  257.8 25.4 %collective-permute-start.7 = (bf16[1024,512]{0,1:T(8,128)(2,1)}, bf16[1024,512]{0,1:T(8,128)(2,1)S(1)}, u32[]{:S(2)}, u32[]{:S(2)}) collective-permute-start(bf16[1024,512]{0,1:T(8,128)(2,1)} %add_convert_fusion.3), channel_id=1, source_target_pairs={{0,2},{1,3},{2,0},{3,1},{4,6},{5,7},{6,4},{7,5},{8,10},{9,11},{10,... | collective-permute-start | bytes 3145736 | tf_op jit(solution)/shard_map/ppermute | solution.py:24
  262.1 21.1 %collective-permute-start.5 = (bf16[1024,512]{0,1:T(8,128)(2,1)}, bf16[1024,512]{0,1:T(8,128)(2,1)}, u32[]{:S(2)}, u32[]{:S(2)}) collective-permute-start(bf16[1024,512]{0,1:T(8,128)(2,1)} %convolution_convert_fusion.4), channel_id=1, source_target_pairs={{0,1},{1,0},{2,3},{3,2},{4,5},{5,4},{6,7},{7,6},{8,9},{9,8},{10,11... | collective-permute-start | bytes 3145736 | tf_op jit(solution)/shard_map/ppermute | solution.py:24
  285.8 24.4 %collective-permute-start.8 = (bf16[1024,512]{0,1:T(8,128)(2,1)S(1)}, bf16[1024,512]{0,1:T(8,128)(2,1)S(1)}, u32[]{:S(2)}, u32[]{:S(2)}) collective-permute-start(bf16[1024,512]{0,1:T(8,128)(2,1)S(1)} %add_convert_fusion.2), channel_id=1, source_target_pairs={{0,2},{1,3},{2,0},{3,1},{4,6},{5,7},{6,4},{7,5},{8,10},{9,11},{10,... | collective-permute-start | bytes 3145736 | tf_op jit(solution)/shard_map/ppermute | solution.py:24
  311.7 13.4 %collective-permute-start.10 = (bf16[1024,512]{0,1:T(8,128)(2,1)}, bf16[1024,512]{0,1:T(8,128)(2,1)}, u32[]{:S(2)}, u32[]{:S(2)}) collective-permute-start(bf16[1024,512]{0,1:T(8,128)(2,1)} %get-tuple-element.45), channel_id=1, source_target_pairs={{0,1},{1,0},{2,3},{3,2},{4,5},{5,4},{6,7},{7,6},{8,9},{9,8},{10,11... | collective-permute-start | bytes 3145736 | tf_op jit(solution)/shard_map/ppermute | solution.py:24
  311.7 15.3 %collective-permute-start.9 = (bf16[1024,512]{0,1:T(8,128)(2,1)}, bf16[1024,512]{0,1:T(8,128)(2,1)}, u32[]{:S(2)}, u32[]{:S(2)}) collective-permute-start(bf16[1024,512]{0,1:T(8,128)(2,1)} %get-tuple-element.44), channel_id=1, source_target_pairs={{0,1},{1,0},{2,3},{3,2},{4,5},{5,4},{6,7},{7,6},{8,9},{9,8},{10,11... | collective-permute-start | bytes 3145736 | tf_op jit(solution)/shard_map/ppermute | solution.py:24
  312.2 116.9 %all-to-all-start.1 = ((bf16[16,4,128,128]{3,2,1,0:T(8,128)(2,1)}), bf16[16,4,128,128]{3,2,1,0:T(8,128)(2,1)S(1)}, u32[]{:S(2)}, u32[]{:S(2)}) async-start(bf16[16,4,128,128]{3,2,1,0:T(8,128)(2,1)} %get-tuple-element.24), calls=%async_computation.1 | async-start | bytes 4194304 | tf_op jit(solution)/shard_map/all_to_all | solution.py:415
  429.1 85.9 %copy-start.15 = (bf16[16,4,128,128]{3,2,1,0:T(8,128)(2,1)}, bf16[16,4,128,128]{3,2,1,0:T(8,128)(2,1)S(1)}, u32[]{:S(2)}) copy-start(bf16[16,4,128,128]{3,2,1,0:T(8,128)(2,1)S(1)} %all-to-all-done.1.x_ref) | copy-start | bytes 6291460
  515.0 2.7 collective-permute-start.12
  517.4 15.3 %collective-permute-start.11 = (bf16[1024,512]{0,1:T(8,128)(2,1)S(1)}, bf16[1024,512]{0,1:T(8,128)(2,1)S(1)}, u32[]{:S(2)}, u32[]{:S(2)}) collective-permute-start(bf16[1024,512]{0,1:T(8,128)(2,1)S(1)} %convolution_convert_fusion.2), channel_id=1, source_target_pairs={{0,1},{1,0},{2,3},{3,2},{4,5},{5,4},{6,7},{7,6},{8,9},{9,8},{10,11... | collective-permute-start | bytes 3145736 | tf_op jit(solution)/shard_map/ppermute | solution.py:24
  520.5 25.7 %collective-permute-start.13 = (bf16[1024,512]{0,1:T(8,128)(2,1)}, bf16[1024,512]{0,1:T(8,128)(2,1)}, u32[]{:S(2)}, u32[]{:S(2)}) collective-permute-start(bf16[1024,512]{0,1:T(8,128)(2,1)} %add_convert_fusion.1), channel_id=1, source_target_pairs={{0,2},{1,3},{2,0},{3,1},{4,6},{5,7},{6,4},{7,5},{8,10},{9,11},{10,... | collective-permute-start | bytes 3145736 | tf_op jit(solution)/shard_map/ppermute | solution.py:24
  (36 other events, 492.3 us)
Sparse Core Ops, SparseCore 0:
  35.3 100.2 all-gather.6
  137.7 47.7 all-gather.14
  187.7 94.0 all-gather.8
  283.9 132.1 all-gather.10
  418.0 92.7 all-gather.12
